TPU v7x, 256 devices: a whole 4x4x8 slice. The times are simulated.
256 devices in a mesh: dp: 4 (over x), ctx: 32 (over y, z), head: 2 (over core).
Axes of the slice: x: 4, y: 4, z: 8, core: 2. Of those that a mesh axis runs over, the one named last changes fastest.
Arguments:
- queries: bfloat16 [16384, 32, 128], P(('dp', 'ctx'), 'head'), parts along dimension 0, may hold values from -15 to 15
- key_rows: bfloat16 [16384, 4, 128], P(('dp', 'ctx'), 'head'), parts along dimension 0, may hold values from -15 to 15
- values: bfloat16 [16384, 4, 128], P(('dp', 'ctx'), 'head'), parts along dimension 0, may hold values from -12 to 12
- out_grad: bfloat16 [16384, 32, 128], P(('dp', 'ctx'), 'head'), parts along dimension 0, may hold values from -6 to 6
- doc_lengths: int32 [64], P('dp'), parts along dimension 0, may hold values from 1 to 3072, 4096 in all
Outputs:
- attended: bfloat16 [16384, 32, 128], P(('dp', 'ctx'), 'head'), parts along dimension 0
- query_grad: bfloat16 [16384, 32, 128], P(('dp', 'ctx'), 'head'), parts along dimension 0
- key_grad: bfloat16 [16384, 4, 128], P(('dp', 'ctx'), 'head'), parts along dimension 0
- value_grad: bfloat16 [16384, 4, 128], P(('dp', 'ctx'), 'head'), parts along dimension 0
There are 4 independent parts, one for each index of `dp`. A program takes and returns all parts, laid end to end along the dimension named above; each array names one. Nothing has to cross between parts.
Inputs may be any that keep to these rules, and one draw needn't show every extreme that they name: `doc_lengths`: the lengths sum to 4096; the longest is exactly 3072.
All inputs are finite; a program needn't handle non-finite values.
Results may differ from a plain program's by a relative error of at most 0.03.
Values may be sent and summed in bfloat16 or wider, within the bound.
No kernel may reach another device: no remote copies, remote signals or barrier semaphores. Data moves between devices by JAX's collectives and lax.ppermute only.
A program may use at most 128 MiB of HBM per device.

v0:
```python
import functools
import math

import jax
import jax.numpy as jnp
from jax import lax
from jax.experimental import pallas as pl
from jax.experimental.pallas import tpu as pltpu
from jax.sharding import PartitionSpec as P

MASKED_SCORE = -1e30
NY, NZ = 4, 8


def dot_tn(left, right):
    return lax.dot_general(left, right, (((0,), (0,)), ((), ())), preferred_element_type=jnp.float32)


def dot_nt(left, right):
    return lax.dot_general(left, right, (((1,), (1,)), ((), ())), preferred_element_type=jnp.float32)


def dot_nn(left, right):
    return jnp.dot(left, right, preferred_element_type=jnp.float32)


def stage_kernel(stage, waits, passing, block, group, *refs):
    kind, forward, finish, backward, last = stage
    first = forward and kind == "own"
    paired = kind == "pair"
    units = 4 if paired else 2
    lanes = block * group
    refs = list(refs)
    take = lambda count: [refs.pop(0) for _ in range(count)]
    take(waits)
    docs_ref, place_ref = take(2)
    q_in = take(2)
    g_in = take(2) if backward else []
    pieces = take(1 if kind == "own" else 2)
    state_in = take(3) if forward and not first else []
    stats_in = take(2) if backward and not finish else []
    dq_in = take(1) if backward and not finish else []
    take(passing)
    state_out = take(3) if forward and not finish else []
    rows_out = take(2) if finish or last else []
    stats_out = take(2) if finish else []
    dq_out = take(1) if backward and not last else []
    grads = take(len(pieces)) if backward else []
    take(passing)
    k_scr, v_scr, q_scr = take(3)
    if finish:
        state_out = take(3)
    if backward:
        g_scr, dk_scr, dv_scr = take(3)
    if last:
        dq_out = take(1)
    stats = stats_out or stats_in

    head_size = q_in[0].shape[1]
    scale = 1.0 / math.sqrt(head_size)
    log2_scale = scale * math.log2(math.e)
    y, z, distance = place_ref[0], place_ref[1], place_ref[2]

    def block_of(slot, steps):
        return (y ^ slot ^ (slot >> 1)) * NZ + lax.rem(z + NZ + steps, NZ)

    def blocks_of(unit):
        if paired:
            return block_of(unit, distance), block_of(unit, -distance)
        return block_of(2 * unit, distance), block_of(2 * unit + 1, distance)

    def places():
        for unit in range(units):
            for half in range(2):
                if paired:
                    yield unit, half, half, unit
                else:
                    yield (unit, half, 0, 2 * unit + half) if kind == "own" else (unit, half, unit, half)

    for unit, half, piece, slot in places():
        rows = pl.ds(half * block, block)
        k_scr[unit, rows, :] = pieces[piece][slot, 0]
        v_scr[unit, rows, :] = pieces[piece][slot, 1]
    for part in range(2):
        q_scr[part] = q_in[part][...]
        if backward:
            g_scr[part] = g_in[part][...]

    def doc_start(position):
        bound, start = jnp.int32(0), jnp.zeros_like(position)
        for number in range(docs_ref.shape[0]):
            bound = bound + docs_ref[number]
            start = jnp.where(bound <= position, bound, start)
        return start

    def fold(value):
        return value.reshape(value.shape[0] // 8, 8, value.shape[1])

    def part_facts(part):
        query_block = jnp.where(part == 0, y, NY - 1 - y) * NZ + z
        first_pos = query_block * block
        return query_block, doc_start(first_pos), doc_start(first_pos + block - 1)

    def is_live(unit, facts):
        query_block, open_first, _ = facts
        return [(n <= query_block) & ((n + 1) * block > open_first) for n in blocks_of(unit)]

    def is_clear(unit, facts):
        query_block, _, open_last = facts
        one, two = ((n < query_block) & (n * block >= open_last) for n in blocks_of(unit))
        return one & two

    def scores_of(unit, rows, part, facts, masked):
        scores = dot_nt(k_scr[unit, rows, :], q_scr[part])
        if masked:
            lane = lax.broadcasted_iota(jnp.int32, (1, lanes), 1)
            positions = facts[0] * block + lane // group
            one, two = blocks_of(unit)
            row = lax.broadcasted_iota(jnp.int32, scores.shape, 0)
            key_pos = row + jnp.where(rows.start == 0, one, two) * block
            allowed = (key_pos <= positions) & (key_pos >= doc_start(positions))
            scores = jnp.where(allowed, scores, MASKED_SCORE)
        return scores

    def each_unit(facts, work):
        def step(unit, _):
            one, two = is_live(unit, facts)
            clear = is_clear(unit, facts) & one & two
            pl.when(clear)(lambda: work(unit, pl.ds(0, 2 * block), False))

            def half_step(half, _):
                live = jnp.where(half == 0, one, two) & jnp.logical_not(clear)
                rows = pl.ds(pl.multiple_of(half * block, block), block)
                pl.when(live)(lambda: work(unit, rows, True))
                return 0

            lax.fori_loop(0, 2, half_step, 0)
            return 0

        lax.fori_loop(0, units, step, 0)

    def forward_part(part, _):
        facts = part_facts(part)
        m_new, l_new, o_new = state_out
        if first:
            m_new[part] = jnp.full((8, lanes), MASKED_SCORE, jnp.float32)
            l_new[part] = jnp.zeros((8, lanes), jnp.float32)
            o_new[part] = jnp.zeros((head_size, lanes), jnp.float32)
        else:
            for old, new in zip(state_in, state_out):
                new[part] = old[part]

        def attend(unit, rows, masked):
            scores = scores_of(unit, rows, part, facts, masked)
            m_old = m_new[part]
            top = jnp.maximum(m_old, jnp.max(scores, axis=0, keepdims=True))
            fading = jnp.exp2((m_old - top) * log2_scale)
            weights = jnp.exp2(scores * log2_scale - top[:1] * log2_scale)
            m_new[part] = top
            l_new[part] = l_new[part] * fading + jnp.sum(fold(weights), axis=0)
            added = dot_tn(v_scr[unit, rows, :], weights.astype(jnp.bfloat16))
            o_new[part] = o_new[part] * fading[:1] + added

        each_unit(facts, attend)
        row_max = m_new[part][:1] * log2_scale
        if finish:
            row_total = jnp.sum(l_new[part], axis=0, keepdims=True)
            attended = (o_new[part] / row_total).T.astype(jnp.bfloat16)
            products = attended.astype(jnp.float32) * g_scr[part].astype(jnp.float32)
            stats_out[0][part] = jnp.broadcast_to(row_max + jnp.log2(row_total), (8, lanes))
            upper = products.astype(jnp.bfloat16)
            lower = (products - upper.astype(jnp.float32)).astype(jnp.bfloat16)
            ones = jnp.ones((8, head_size), jnp.bfloat16)
            stats_out[1][part] = dot_nt(ones, upper) + dot_nt(ones, lower)
            write_rows(part, attended)
        return 0

    def write_rows(part, rows):
        for number in range(2):

            @pl.when(part == number)
            def _():
                rows_out[number][...] = rows

    def backward_part(part, _):
        facts = part_facts(part)
        log_total, out_dot = stats[0][part][:1], stats[1][part][:1]
        dq_new = dq_out[0]
        dq_new[part] = jnp.zeros((head_size, lanes), jnp.float32) if finish else dq_in[0][part]

        def differentiate(unit, rows, masked):
            probs = jnp.exp2(scores_of(unit, rows, part, facts, masked) * log2_scale - log_total)
            dprobs = dot_nt(v_scr[unit, rows, :], g_scr[part])
            dscores = (probs * (dprobs - out_dot)).astype(jnp.bfloat16)
            dv_scr[unit, rows, :] += dot_nn(probs.astype(jnp.bfloat16), g_scr[part])
            dk_scr[unit, rows, :] += dot_nn(dscores, q_scr[part])
            dq_new[part] += dot_tn(k_scr[unit, rows, :], dscores)

        each_unit(facts, differentiate)
        if last:
            write_rows(part, (dq_new[part] * scale).T.astype(jnp.bfloat16))
        return 0

    if forward:
        lax.fori_loop(0, 2, forward_part, 0)
    if backward:
        dk_scr[...] = jnp.zeros_like(dk_scr)
        dv_scr[...] = jnp.zeros_like(dv_scr)
        lax.fori_loop(0, 2, backward_part, 0)
        for unit, half, piece, slot in places():
            rows = pl.ds(half * block, block)
            grads[piece][slot, 0] = (dk_scr[unit, rows, :] * scale).astype(jnp.bfloat16)
            grads[piece][slot, 1] = dv_scr[unit, rows, :].astype(jnp.bfloat16)


def run_stage(step, phases, block, group, docs, spot, q_parts, g_parts, pieces, state=(), stats=(), dq=(), after=(), passing=()):
    forward, finish, backward, last = phases
    kind = {0: "own", 4: "far"}.get(step, "pair")
    stage = (kind, *phases)
    units = 4 if kind == "pair" else 2
    y, z = spot
    place = jnp.stack([y, z, jnp.where(z % 2 == 0, step, -step)]).astype(jnp.int32)
    lanes, head_size = q_parts[0].shape
    f32 = lambda *shape: jax.ShapeDtypeStruct(shape, jnp.float32)
    low = lambda array: jax.ShapeDtypeStruct(array.shape, jnp.bfloat16)
    state_shapes = [f32(2, 8, lanes), f32(2, 8, lanes), f32(2, head_size, lanes)]
    dq_shape = f32(2, head_size, lanes)
    operands = [*after, docs, place, *q_parts, *(g_parts if backward else ()), *pieces, *state, *stats, *dq, *passing]
    outs = []
    aliases = {}
    if forward and not finish:
        if state:
            aliases = {len(operands) - 3 + n: n for n in range(3)}
        outs += state_shapes
    if finish or last:
        outs += [low(q) for q in q_parts]
    if finish:
        outs += state_shapes[:2]
    if backward and not last:
        if dq:
            aliases = {len(operands) - 1: len(outs)}
        outs += [dq_shape]
    if backward:
        outs += [low(piece) for piece in pieces]
    for number, array in enumerate(passing):
        aliases[len(operands) - len(passing) + number] = len(outs)
        outs += [low(array)]
    scratch = [
        pltpu.VMEM((units, 2 * block, head_size), jnp.bfloat16),
        pltpu.VMEM((units, 2 * block, head_size), jnp.bfloat16),
        pltpu.VMEM((2, lanes, head_size), jnp.bfloat16),
    ]
    if finish:
        scratch += [pltpu.VMEM(shape.shape, jnp.float32) for shape in state_shapes]
    if backward:
        scratch += [
            pltpu.VMEM((2, lanes, head_size), jnp.bfloat16),
            pltpu.VMEM((units, 2 * block, head_size), jnp.float32),
            pltpu.VMEM((units, 2 * block, head_size), jnp.float32),
        ]
    if last:
        scratch += [pltpu.VMEM(dq_shape.shape, jnp.float32)]
    smem = pl.BlockSpec(memory_space=pltpu.SMEM)
    vmem = pl.BlockSpec(memory_space=pltpu.VMEM)
    anywhere = pl.BlockSpec(memory_space=pl.ANY)
    inside = len(operands) - 2 - len(after) - len(passing)
    products = 2 * forward + 5 * backward
    return pl.pallas_call(
        functools.partial(stage_kernel, stage, len(after), len(passing), block, group),
        out_shape=outs,
        in_specs=[anywhere] * len(after) + [smem, smem] + [vmem] * inside + [anywhere] * len(passing),
        out_specs=[vmem] * (len(outs) - len(passing)) + [anywhere] * len(passing),
        scratch_shapes=scratch,
        input_output_aliases=aliases,
        compiler_params=pltpu.CompilerParams(vmem_limit_bytes=24 * 1024 * 1024),
        cost_estimate=pl.CostEstimate(
            flops=6 * products * 2 * lanes * units * 2 * block * head_size,
            bytes_accessed=4 * 1024 * 1024,
            transcendentals=2 * lanes * units * 2 * block,
        ),
        name="fwd" * forward + "bwd" * backward + kind,
    )(*operands)


def swap_y(mask):
    return [(y * NZ + z, (y ^ mask) * NZ + z) for y in range(NY) for z in range(NZ)]


def swap_z(first):
    turns = [1 if z % 2 == first else -1 for z in range(NZ)]
    return [(y * NZ + z, y * NZ + (z + turns[z]) % NZ) for y in range(NY) for z in range(NZ)]


MIRROR = swap_y(NY - 1)


def add_up(one, other):
    return (one.astype(jnp.float32) + other.astype(jnp.float32)).astype(jnp.bfloat16)


def swap_even(array):
    return lax.ppermute(array, "ctx", swap_z(0))


def swap_odd(array):
    return lax.ppermute(array, "ctx", swap_z(1))


def on_device(queries, key_rows, values, out_grad, doc_lengths):
    block, query_heads, head_size = queries.shape
    key_heads = key_rows.shape[1]
    group = query_heads // key_heads
    place = lax.axis_index("ctx")
    y, z = place // NZ, place % NZ
    mine = y // 2

    def head_of(array, number, width):
        picked = jnp.where(number == 0, array[:, :width], array[:, width:])
        return picked.reshape(block * width, head_size)

    def key_pair(number):
        return jnp.stack([head_of(key_rows, number, 1), head_of(values, number, 1)])

    pairs = [key_pair(mine), key_pair(1 - mine)]
    held = [lax.ppermute(pairs[mask // 2], "ctx", swap_y(mask)) for mask in (1, 3, 2)]
    column = jnp.stack([pairs[0], *held])

    q_parts = [head_of(queries, mine, group), lax.ppermute(head_of(queries, 1 - mine, group), "ctx", MIRROR)]
    g_own, g_leaving = head_of(out_grad, mine, group), head_of(out_grad, 1 - mine, group)
    run = functools.partial(
        run_stage, block=block, group=group, docs=doc_lengths, spot=(y, z), q_parts=q_parts
    )

    evens, odds = [column], [column]
    state = ()
    for step in range(4):
        pieces = [column] if step == 0 else [evens[step], odds[step]]
        if step < 3:
            even, odd = swap_even(odds[step]), swap_odd(evens[step])
        else:
            even, odd = swap_even(odds[step][:2]), swap_odd(evens[step][2:])
        evens.append(even)
        odds.append(odd)
        passing = () if step else (g_leaving,)
        state = run(step, (True, False, False, False), g_parts=(), pieces=pieces, state=state, passing=passing)
        if passing:
            g_parts = [g_own, lax.ppermute(state[3], "ctx", MIRROR)]
            state = state[:3]
    run = functools.partial(run, g_parts=g_parts)
    own_out, other_out, log_total, out_dot, dq, even_grad, odd_grad = run(
        4, (True, True, True, False), pieces=[evens[4], odds[4]], state=state
    )
    stats = (log_total, out_dot)
    other_out = lax.ppermute(other_out, "ctx", MIRROR)
    even, odd = swap_even(even_grad), swap_odd(odd_grad)
    after = ()
    for step in (3, 2, 1):
        dq, even_grad, odd_grad = run(
            step, (False, False, True, False), pieces=[evens[step], odds[step]], stats=stats, dq=(dq,), after=after
        )
        if step == 3:
            odd_grad = jnp.concatenate([add_up(odd_grad[:2], even), odd_grad[2:]], axis=0)
            even_grad = jnp.concatenate([even_grad[:2], add_up(even_grad[2:], odd)], axis=0)
        else:
            odd_grad, even_grad = add_up(odd_grad, even), add_up(even_grad, odd)
        after = (even_grad, odd_grad)
        even, odd = swap_even(even_grad), swap_odd(odd_grad)
    own_dq, other_dq, grad, other_out = run(
        0, (False, False, True, True), pieces=[column], stats=stats, dq=(dq,), after=after, passing=(other_out,)
    )
    other_dq = lax.ppermute(other_dq, "ctx", MIRROR)
    sums = grad.astype(jnp.float32) + even.astype(jnp.float32) + odd.astype(jnp.float32)

    def both_heads(own, other):
        one, two = (r.reshape(block, group, head_size) for r in (own, other))
        return jnp.concatenate([jnp.where(mine == 0, one, two), jnp.where(mine == 0, two, one)], axis=1)

    attended, query_grad = both_heads(own_out, other_out), both_heads(own_dq, other_dq)
    arrived = {
        mask: lax.ppermute(sums[slot].astype(jnp.bfloat16), "ctx", swap_y(mask)).astype(jnp.float32)
        for slot, mask in ((3, 2), (2, 3), (1, 1))
    }
    near, far = sums[0] + arrived[1], arrived[2] + arrived[3]
    heads = [jnp.where(mine == 0, near, far), jnp.where(mine == 0, far, near)]
    grads = jnp.stack(heads, axis=2).astype(jnp.bfloat16)
    return attended, query_grad, grads[0], grads[1]


def solution(mesh):
    placed = (
        P(("dp", "ctx"), "head", None),
        P(("dp", "ctx"), "head", None),
        P(("dp", "ctx"), "head", None),
        P(("dp", "ctx"), "head", None),
        P("dp"),
    )
    return jax.shard_map(
        on_device,
        mesh=mesh,
        in_specs=placed,
        out_specs=(
            P(("dp", "ctx"), "head", None),
            P(("dp", "ctx"), "head", None),
            P(("dp", "ctx"), "head", None),
            P(("dp", "ctx"), "head", None),
        ),
        check_vma=False,
    )
```

profile of v0, /device:TPU:6, one launch (start us, length us, event | category | flops | bytes accessed | tf_op | source)
XLA Modules:
  0.0 98.5 jit_solution(1337050922096621147)
XLA Ops:
  2.5 3.3 %collective-permute-start.3 = (bf16[2,128,128]{2,1,0:T(8,128)(2,1)S(1)}, bf16[2,128,128]{2,1,0:T(8,128)(2,1)S(1)}, u32[]{:S(2)}, u32[]{:S(2)}) collective-permute-start(bf16[2,128,128]{2,1,0:T(8,128)(2,1)S(1)} %pad_maximum_fusion.7), channel_id=1, source_target_pairs={{0,32},{2,34},{4,36},{6,38},{8,40},{10,42},{12,44},{14,46},{16,48}... | collective-permute-start | bytes 196616 | tf_op jit(solution)/shard_map/ppermute | solution.py:325
  7.0 2.3 %collective-permute-start = (bf16[1024,128]{1,0:T(8,128)(2,1)S(1)}, bf16[1024,128]{1,0:T(8,128)(2,1)S(1)}, u32[]{:S(2)}, u32[]{:S(2)}) collective-permute-start(bf16[1024,128]{1,0:T(8,128)(2,1)S(1)} %get-tuple-element.86), channel_id=1, source_target_pairs={{0,48},{2,50},{4,52},{6,54},{8,56},{10,58},{12,60},{14,62},{16,32}... | collective-permute-start | bytes 786440 | tf_op jit(solution)/shard_map/ppermute | solution.py:328
  9.4 1.7 %collective-permute-done.1 = bf16[2,128,128]{2,1,0:T(8,128)(2,1)S(1)} collective-permute-done((bf16[2,128,128]{2,1,0:T(8,128)(2,1)S(1)}, bf16[2,128,128]{2,1,0:T(8,128)(2,1)S(1)}, u32[]{:S(2)}, u32[]{:S(2)}) %collective-permute-start.1) | collective-permute-done | bytes 65568 | tf_op jit(solution)/shard_map/ppermute | solution.py:325
  11.9 2.0 %collective-permute-start.9 = (bf16[4,2,128,128]{3,2,1,0:T(8,128)(2,1)S(1)}, bf16[4,2,128,128]{3,2,1,0:T(8,128)(2,1)S(1)}, u32[]{:S(2)}, u32[]{:S(2)}) collective-permute-start(bf16[4,2,128,128]{3,2,1,0:T(8,128)(2,1)S(1)} %pad_maximum_fusion.2.refs_4_.refs_8_), channel_id=1, source_target_pairs={{0,2},{2,0},{4,6},{6,4},{8,10},{10,8},{12,14},{14,12},{16,18},{18,... | collective-permute-start | bytes 786440 | tf_op jit(solution)/shard_map/ppermute | solution.py:302
  13.9 4.9 %collective-permute-start.5 = (bf16[4,2,128,128]{3,2,1,0:T(8,128)(2,1)S(1)}, bf16[4,2,128,128]{3,2,1,0:T(8,128)(2,1)S(1)}, u32[]{:S(2)}, u32[]{:S(2)}) collective-permute-start(bf16[4,2,128,128]{3,2,1,0:T(8,128)(2,1)S(1)} %pad_maximum_fusion.2.refs_4_.refs_8_), channel_id=1, source_target_pairs={{0,14},{2,4},{4,2},{6,8},{8,6},{10,12},{12,10},{14,0},{16,30},{18,... | collective-permute-start | bytes 786440 | tf_op jit(solution)/shard_map/ppermute | solution.py:306
  19.6 3.0 %fwdown.1 = (f32[2,8,1024]{2,1,0:T(8,128)S(1)}, f32[2,8,1024]{2,1,0:T(8,128)S(1)}, f32[2,128,1024]{2,1,0:T(8,128)S(1)}, bf16[1024,128]{1,0:T(8,128)(2,1)S(1)}) custom-call(s32[16]{0:T(128)S(1)} %copy-done, s32[3]{0:T(128)S(1)} %get-tuple-element.105.refs_1_.refs_3_, ...), custom_call_target="tpu_custom_call", output_to_operand_aliasing={{3}: (5, {})} | custom-call | flops 1610612736 | bytes 4194304 | tf_op jit(solution)/shard_map/fwdown/pallas_call | solution.py:268
  24.2 2.3 %collective-permute-start.10 = (bf16[4,2,128,128]{3,2,1,0:T(8,128)(2,1)S(1)}, bf16[4,2,128,128]{3,2,1,0:T(8,128)(2,1)S(1)}, u32[]{:S(2)}, u32[]{:S(2)}) collective-permute-start(bf16[4,2,128,128]{3,2,1,0:T(8,128)(2,1)S(1)} %collective-permute-done.9.refs_4_.refs_8_), channel_id=1, source_target_pairs={{0,14},{2,4},{4,2},{6,8},{8,6},{10,12},{12,10},{14,0},{16,30},{18,... | collective-permute-start | bytes 786440 | tf_op jit(solution)/shard_map/ppermute | solution.py:306
  26.5 3.6 %fwdpair.3 = (f32[2,8,1024]{2,1,0:T(8,128)S(1)}, f32[2,8,1024]{2,1,0:T(8,128)S(1)}, f32[2,128,1024]{2,1,0:T(8,128)S(1)}) custom-call(s32[16]{0:T(128)S(1)} %copy-done, s32[3]{0:T(128)S(1)} %get-tuple-element.76.refs_1_.refs_3_, bf16[1024,128]{1,0:T(8,128)(2,1)S(1)} %get-tuple-element.87.refs_2_.refs_4_, ...), custom_call_target="tpu_custom_call", output_to_operand_aliasing={{0}: (6, {}), {1}: (7, {}), {2}: (8, {})} | custom-call | flops 3221225472 | bytes 4194304 | tf_op jit(solution)/shard_map/fwdpair/pallas_call | solution.py:268
  34.1 3.2 %fwdpair.4 = (f32[2,8,1024]{2,1,0:T(8,128)S(1)}, f32[2,8,1024]{2,1,0:T(8,128)S(1)}, f32[2,128,1024]{2,1,0:T(8,128)S(1)}) custom-call(s32[16]{0:T(128)S(1)} %copy-done, s32[3]{0:T(128)S(1)} %get-tuple-element.103.refs_1_.refs_3_, bf16[1024,128]{1,0:T(8,128)(2,1)S(1)} %get-tuple-element.87.refs_2_.refs_4_, ...), custom_call_target="tpu_custom_call", output_to_operand_aliasing={{0}: (6, {}), {1}: (7, {}), {2}: (8, {})} | custom-call | flops 3221225472 | bytes 4194304 | tf_op jit(solution)/shard_map/fwdpair/pallas_call | solution.py:268
  38.5 2.0 %collective-permute-start.12 = (bf16[2,2,128,128]{3,2,1,0:T(8,128)(2,1)S(1)}, bf16[2,2,128,128]{3,2,1,0:T(8,128)(2,1)S(1)}, u32[]{:S(2)}, u32[]{:S(2)}) collective-permute-start(bf16[2,2,128,128]{3,2,1,0:T(8,128)(2,1)S(1)} %slice.92), channel_id=1, source_target_pairs={{0,14},{2,4},{4,2},{6,8},{8,6},{10,12},{12,10},{14,0},{16,30},{18,... | collective-permute-start | bytes 393224 | tf_op jit(solution)/shard_map/ppermute | solution.py:306
  40.6 2.3 %collective-permute-done.7.refs_5_.refs_7_ = bf16[4,2,128,128]{3,2,1,0:T(8,128)(2,1)S(1)} collective-permute-done((bf16[4,2,128,128]{3,2,1,0:T(8,128)(2,1)S(1)}, bf16[4,2,128,128]{3,2,1,0:T(8,128)(2,1)S(1)}, u32[]{:S(2)}, u32[]{:S(2)}) %collective-permute-start.7) | collective-permute-done | bytes 262176 | tf_op jit(solution)/shard_map/ppermute | solution.py:306
  43.2 3.2 %fwdpair.5 = (f32[2,8,1024]{2,1,0:T(8,128)S(1)}, f32[2,8,1024]{2,1,0:T(8,128)S(1)}, f32[2,128,1024]{2,1,0:T(8,128)S(1)}) custom-call(s32[16]{0:T(128)S(1)} %copy-done, s32[3]{0:T(128)S(1)} %get-tuple-element.104.refs_1_, bf16[1024,128]{1,0:T(8,128)(2,1)S(1)} %get-tuple-element.87.refs_2_.refs_4_, ...), custom_call_target="tpu_custom_call", output_to_operand_aliasing={{0}: (6, {}), {1}: (7, {}), {2}: (8, {})} | custom-call | flops 3221225472 | bytes 4194304 | tf_op jit(solution)/shard_map/fwdpair/pallas_call | solution.py:268
  46.4 1.7 %collective-permute-done.8.refs_6_ = bf16[2,2,128,128]{3,2,1,0:T(8,128)(2,1)S(1)} collective-permute-done((bf16[2,2,128,128]{3,2,1,0:T(8,128)(2,1)S(1)}, bf16[2,2,128,128]{3,2,1,0:T(8,128)(2,1)S(1)}, u32[]{:S(2)}, u32[]{:S(2)}) %collective-permute-start.8) | collective-permute-done | bytes 131104 | tf_op jit(solution)/shard_map/ppermute | solution.py:302
  48.2 4.7 %fwdbwdfar.1 = (bf16[1024,128]{1,0:T(8,128)(2,1)S(1)}, bf16[1024,128]{1,0:T(8,128)(2,1)S(1)}, f32[2,8,1024]{2,1,0:T(8,128)S(1)}, f32[2,8,1024]{2,1,0:T(8,128)S(1...) custom-call(s32[16]{0:T(128)S(1)} %copy-done, ...), custom_call_target="tpu_custom_call" | custom-call | flops 5637144576 | bytes 4194304 | tf_op jit(solution)/shard_map/fwdbwdfar/pallas_call | solution.py:268
  53.0 2.3 %collective-permute-start.14 = (bf16[2,2,128,128]{3,2,1,0:T(8,128)(2,1)S(1)}, bf16[2,2,128,128]{3,2,1,0:T(8,128)(2,1)S(1)}, u32[]{:S(2)}, u32[]{:S(2)}) collective-permute-start(bf16[2,2,128,128]{3,2,1,0:T(8,128)(2,1)S(1)} %get-tuple-element.57), channel_id=1, source_target_pairs={{0,2},{2,0},{4,6},{6,4},{8,10},{10,8},{12,14},{14,12},{16,18},{18,... | collective-permute-start | bytes 393224 | tf_op jit(solution)/shard_map/ppermute | solution.py:302
  56.2 3.7 %bwdpair.3 = (f32[2,128,1024]{2,1,0:T(8,128)S(1)}, bf16[4,2,128,128]{3,2,1,0:T(8,128)(2,1)S(1)}, bf16[4,2,128,128]{3,2,1,0:T(8,128)(2,1)S(1)}) custom-call(s32[16]{0:T(128)S(1)} %copy-done, s32[3]{0:T(128)S(1)} %get-tuple-element.104.refs_1_, bf16[1024,128]{1,0:T(8,128)(2,1)S(1)} %get-tuple-element.87.refs_2_.refs_4_, ...), custom_call_target="tpu_custom_call", output_to_operand_aliasing={{0}: (10, {})} | custom-call | flops 8053063680 | bytes 4194304 | tf_op jit(solution)/shard_map/bwdpair/pallas_call | solution.py:268
  61.8 1.7 %collective-permute-start.16 = (bf16[4,2,128,128]{3,2,1,0:T(8,128)(2,1)S(1)}, bf16[4,2,128,128]{3,2,1,0:T(8,128)(2,1)S(1)}, u32[]{:S(2)}, u32[]{:S(2)}) collective-permute-start(bf16[4,2,128,128]{3,2,1,0:T(8,128)(2,1)S(1)} %pad_maximum_fusion.3.refs_0_), channel_id=1, source_target_pairs={{0,2},{2,0},{4,6},{6,4},{8,10},{10,8},{12,14},{14,12},{16,18},{18,... | collective-permute-start | bytes 786440 | tf_op jit(solution)/shard_map/ppermute | solution.py:302
  63.5 3.7 %bwdpair.4 = (f32[2,128,1024]{2,1,0:T(8,128)S(1)}, bf16[4,2,128,128]{3,2,1,0:T(8,128)(2,1)S(1)}, bf16[4,2,128,128]{3,2,1,0:T(8,128)(2,1)S(1)}) custom-call(bf16[4,2,128,128]{3,2,1,0:T(8,128)(2,1)S(1)} %pad_maximum_fusion.3.refs_0_, bf16[4,2,128,128]{3,2,1,0:T(8,128)(2,1)S(1)} %pad_maximum_fusion.4.refs_1_, ...), custom_call_target="tpu_custom_call", output_to_operand_aliasing={{0}: (12, {})} | custom-call | flops 8053063680 | bytes 4194304 | tf_op jit(solution)/shard_map/bwdpair/pallas_call | solution.py:268
  71.1 4.1 %bwdpair.5 = (f32[2,128,1024]{2,1,0:T(8,128)S(1)}, bf16[4,2,128,128]{3,2,1,0:T(8,128)(2,1)S(1)}, bf16[4,2,128,128]{3,2,1,0:T(8,128)(2,1)S(1)}) custom-call(bf16[4,2,128,128]{3,2,1,0:T(8,128)(2,1)S(1)} %add_convert_fusion.3.refs_0_, bf16[4,2,128,128]{3,2,1,0:T(8,128)(2,1)S(1)} %add_convert_fusion.2.refs_1_, ...), custom_call_target="tpu_custom_call", output_to_operand_aliasing={{0}: (12, {})} | custom-call | flops 8053063680 | bytes 4194304 | tf_op jit(solution)/shard_map/bwdpair/pallas_call | solution.py:268
  76.5 1.8 %collective-permute-start.22 = (bf16[4,2,128,128]{3,2,1,0:T(8,128)(2,1)S(1)}, bf16[4,2,128,128]{3,2,1,0:T(8,128)(2,1)S(1)}, u32[]{:S(2)}, u32[]{:S(2)}) collective-permute-start(bf16[4,2,128,128]{3,2,1,0:T(8,128)(2,1)S(1)} %add_convert_fusion.refs_1_), channel_id=1, source_target_pairs={{0,14},{2,4},{4,2},{6,8},{8,6},{10,12},{12,10},{14,0},{16,30},{18,... | collective-permute-start | bytes 786440 | tf_op jit(solution)/shard_map/ppermute | solution.py:306
  81.1 3.7 %bwdown.1 = (bf16[1024,128]{1,0:T(8,128)(2,1)S(1)}, bf16[1024,128]{1,0:T(8,128)(2,1)S(1)}, bf16[4,2,128,128]{3,2,1,0:T(8,128)(2,1)S(1)}, bf16[1024,128]{1,0:T(8,128)(2,1)S(1)}) custom-call(bf16[4,2,128,128]{3,2,1,0:T(8,128)(2,1)S(1)} %add_convert_fusion.1.refs_0_, ...), custom_call_target="tpu_custom_call", output_to_operand_aliasing={{3}: (12, {})} | custom-call | flops 4026531840 | bytes 4194304 | tf_op jit(solution)/shard_map/bwdown/pallas_call | solution.py:268
  86.5 2.7 %collective-permute-start.23 = (bf16[2,128,128]{2,1,0:T(8,128)(2,1)S(1)}, bf16[2,128,128]{2,1,0:T(8,128)(2,1)S(1)}, u32[]{:S(2)}, u32[]{:S(2)}) collective-permute-start(bf16[2,128,128]{2,1,0:T(8,128)(2,1)S(1)} %get-tuple-element.88), channel_id=1, source_target_pairs={{0,16},{2,18},{4,20},{6,22},{8,24},{10,26},{12,28},{14,30},{16,0},... | collective-permute-start | bytes 196616 | tf_op jit(solution)/shard_map/ppermute | solution.py:380
  89.2 2.0 %collective-permute-start.25 = (bf16[2,128,128]{2,1,0:T(8,128)(2,1)S(1)}, bf16[2,128,128]{2,1,0:T(8,128)(2,1)S(1)}, u32[]{:S(2)}, u32[]{:S(2)}) collective-permute-start(bf16[2,128,128]{2,1,0:T(8,128)(2,1)S(1)} %get-tuple-element.89), channel_id=1, source_target_pairs={{0,48},{2,50},{4,52},{6,54},{8,56},{10,58},{12,60},{14,62},{16,32}... | collective-permute-start | bytes 196616 | tf_op jit(solution)/shard_map/ppermute | solution.py:380
  94.7 2.3 %collective-permute-done.24 = bf16[2,128,128]{2,1,0:T(8,128)(2,1)S(1)} collective-permute-done((bf16[2,128,128]{2,1,0:T(8,128)(2,1)S(1)}, bf16[2,128,128]{2,1,0:T(8,128)(2,1)S(1)}, u32[]{:S(2)}, u32[]{:S(2)}) %collective-permute-start.24) | collective-permute-done | bytes 65568 | tf_op jit(solution)/shard_map/ppermute | solution.py:380
  (79 shorter events, 29.0 us)
Async XLA Ops:
  2.5 8.7 %collective-permute-start.3 = (bf16[2,128,128]{2,1,0:T(8,128)(2,1)S(1)}, bf16[2,128,128]{2,1,0:T(8,128)(2,1)S(1)}, u32[]{:S(2)}, u32[]{:S(2)}) collective-permute-start(bf16[2,128,128]{2,1,0:T(8,128)(2,1)S(1)} %pad_maximum_fusion.7), channel_id=1, source_target_pairs={{0,32},{2,34},{4,36},{6,38},{8,40},{10,42},{12,44},{14,46},{16,48}... | collective-permute-start | bytes 196616 | tf_op jit(solution)/shard_map/ppermute | solution.py:325
  5.7 6.1 %collective-permute-start.2 = (bf16[2,128,128]{2,1,0:T(8,128)(2,1)S(1)}, bf16[2,128,128]{2,1,0:T(8,128)(2,1)S(1)}, u32[]{:S(2)}, u32[]{:S(2)}) collective-permute-start(bf16[2,128,128]{2,1,0:T(8,128)(2,1)S(1)} %pad_maximum_fusion.7), channel_id=1, source_target_pairs={{0,48},{2,50},{4,52},{6,54},{8,56},{10,58},{12,60},{14,62},{16,32}... | collective-permute-start | bytes 196616 | tf_op jit(solution)/shard_map/ppermute | solution.py:325
  7.0 11.9 %collective-permute-start = (bf16[1024,128]{1,0:T(8,128)(2,1)S(1)}, bf16[1024,128]{1,0:T(8,128)(2,1)S(1)}, u32[]{:S(2)}, u32[]{:S(2)}) collective-permute-start(bf16[1024,128]{1,0:T(8,128)(2,1)S(1)} %get-tuple-element.86), channel_id=1, source_target_pairs={{0,48},{2,50},{4,52},{6,54},{8,56},{10,58},{12,60},{14,62},{16,32}... | collective-permute-start | bytes 786440 | tf_op jit(solution)/shard_map/ppermute | solution.py:328
  11.9 12.3 %collective-permute-start.9 = (bf16[4,2,128,128]{3,2,1,0:T(8,128)(2,1)S(1)}, bf16[4,2,128,128]{3,2,1,0:T(8,128)(2,1)S(1)}, u32[]{:S(2)}, u32[]{:S(2)}) collective-permute-start(bf16[4,2,128,128]{3,2,1,0:T(8,128)(2,1)S(1)} %pad_maximum_fusion.2.refs_4_.refs_8_), channel_id=1, source_target_pairs={{0,2},{2,0},{4,6},{6,4},{8,10},{10,8},{12,14},{14,12},{16,18},{18,... | collective-permute-start | bytes 786440 | tf_op jit(solution)/shard_map/ppermute | solution.py:302
  13.9 12.6 %collective-permute-start.5 = (bf16[4,2,128,128]{3,2,1,0:T(8,128)(2,1)S(1)}, bf16[4,2,128,128]{3,2,1,0:T(8,128)(2,1)S(1)}, u32[]{:S(2)}, u32[]{:S(2)}) collective-permute-start(bf16[4,2,128,128]{3,2,1,0:T(8,128)(2,1)S(1)} %pad_maximum_fusion.2.refs_4_.refs_8_), channel_id=1, source_target_pairs={{0,14},{2,4},{4,2},{6,8},{8,6},{10,12},{12,10},{14,0},{16,30},{18,... | collective-permute-start | bytes 786440 | tf_op jit(solution)/shard_map/ppermute | solution.py:306
  22.5 23.9 %collective-permute-start.4 = (bf16[1024,128]{1,0:T(8,128)(2,1)S(1)}, bf16[1024,128]{1,0:T(8,128)(2,1)S(1)}, u32[]{:S(2)}, u32[]{:S(2)}) collective-permute-start(bf16[1024,128]{1,0:T(8,128)(2,1)S(1)} %get-tuple-element.37), channel_id=1, source_target_pairs={{0,48},{2,50},{4,52},{6,54},{8,56},{10,58},{12,60},{14,62},{16,32}... | collective-permute-start | bytes 786440 | tf_op jit(solution)/shard_map/ppermute | solution.py:347
  24.2 7.6 %collective-permute-start.10 = (bf16[4,2,128,128]{3,2,1,0:T(8,128)(2,1)S(1)}, bf16[4,2,128,128]{3,2,1,0:T(8,128)(2,1)S(1)}, u32[]{:S(2)}, u32[]{:S(2)}) collective-permute-start(bf16[4,2,128,128]{3,2,1,0:T(8,128)(2,1)S(1)} %collective-permute-done.9.refs_4_.refs_8_), channel_id=1, source_target_pairs={{0,14},{2,4},{4,2},{6,8},{8,6},{10,12},{12,10},{14,0},{16,30},{18,... | collective-permute-start | bytes 786440 | tf_op jit(solution)/shard_map/ppermute | solution.py:306
  26.5 7.4 %collective-permute-start.6 = (bf16[4,2,128,128]{3,2,1,0:T(8,128)(2,1)S(1)}, bf16[4,2,128,128]{3,2,1,0:T(8,128)(2,1)S(1)}, u32[]{:S(2)}, u32[]{:S(2)}) collective-permute-start(bf16[4,2,128,128]{3,2,1,0:T(8,128)(2,1)S(1)} %collective-permute-done.5.refs_5_.refs_9_), channel_id=1, source_target_pairs={{0,2},{2,0},{4,6},{6,4},{8,10},{10,8},{12,14},{14,12},{16,18},{18,... | collective-permute-start | bytes 786440 | tf_op jit(solution)/shard_map/ppermute | solution.py:302
  31.8 6.7 %collective-permute-start.11 = (bf16[4,2,128,128]{3,2,1,0:T(8,128)(2,1)S(1)}, bf16[4,2,128,128]{3,2,1,0:T(8,128)(2,1)S(1)}, u32[]{:S(2)}, u32[]{:S(2)}) collective-permute-start(bf16[4,2,128,128]{3,2,1,0:T(8,128)(2,1)S(1)} %collective-permute-done.10.refs_5_.refs_9_), channel_id=1, source_target_pairs={{0,2},{2,0},{4,6},{6,4},{8,10},{10,8},{12,14},{14,12},{16,18},{18,... | collective-permute-start | bytes 786440 | tf_op jit(solution)/shard_map/ppermute | solution.py:302
  33.9 9.0 %collective-permute-start.7 = (bf16[4,2,128,128]{3,2,1,0:T(8,128)(2,1)S(1)}, bf16[4,2,128,128]{3,2,1,0:T(8,128)(2,1)S(1)}, u32[]{:S(2)}, u32[]{:S(2)}) collective-permute-start(bf16[4,2,128,128]{3,2,1,0:T(8,128)(2,1)S(1)} %collective-permute-done.6.refs_4_.refs_8_), channel_id=1, source_target_pairs={{0,14},{2,4},{4,2},{6,8},{8,6},{10,12},{12,10},{14,0},{16,30},{18,... | collective-permute-start | bytes 786440 | tf_op jit(solution)/shard_map/ppermute | solution.py:306
  38.5 7.9 %collective-permute-start.12 = (bf16[2,2,128,128]{3,2,1,0:T(8,128)(2,1)S(1)}, bf16[2,2,128,128]{3,2,1,0:T(8,128)(2,1)S(1)}, u32[]{:S(2)}, u32[]{:S(2)}) collective-permute-start(bf16[2,2,128,128]{3,2,1,0:T(8,128)(2,1)S(1)} %slice.92), channel_id=1, source_target_pairs={{0,14},{2,4},{4,2},{6,8},{8,6},{10,12},{12,10},{14,0},{16,30},{18,... | collective-permute-start | bytes 393224 | tf_op jit(solution)/shard_map/ppermute | solution.py:306
  52.9 8.9 %collective-permute-start.13 = (bf16[2,2,128,128]{3,2,1,0:T(8,128)(2,1)S(1)}, bf16[2,2,128,128]{3,2,1,0:T(8,128)(2,1)S(1)}, u32[]{:S(2)}, u32[]{:S(2)}) collective-permute-start(bf16[2,2,128,128]{3,2,1,0:T(8,128)(2,1)S(1)} %get-tuple-element.55), channel_id=1, source_target_pairs={{0,14},{2,4},{4,2},{6,8},{8,6},{10,12},{12,10},{14,0},{16,30},{18,... | collective-permute-start | bytes 393224 | tf_op jit(solution)/shard_map/ppermute | solution.py:306
  53.0 7.0 %collective-permute-start.14 = (bf16[2,2,128,128]{3,2,1,0:T(8,128)(2,1)S(1)}, bf16[2,2,128,128]{3,2,1,0:T(8,128)(2,1)S(1)}, u32[]{:S(2)}, u32[]{:S(2)}) collective-permute-start(bf16[2,2,128,128]{3,2,1,0:T(8,128)(2,1)S(1)} %get-tuple-element.57), channel_id=1, source_target_pairs={{0,2},{2,0},{4,6},{6,4},{8,10},{10,8},{12,14},{14,12},{16,18},{18,... | collective-permute-start | bytes 393224 | tf_op jit(solution)/shard_map/ppermute | solution.py:302
  55.2 25.9 %collective-permute-start.19 = (bf16[1024,128]{1,0:T(8,128)(2,1)S(1)}, bf16[1024,128]{1,0:T(8,128)(2,1)S(1)}, u32[]{:S(2)}, u32[]{:S(2)}) collective-permute-start(bf16[1024,128]{1,0:T(8,128)(2,1)S(1)} %get-tuple-element.65), channel_id=1, source_target_pairs={{0,48},{2,50},{4,52},{6,54},{8,56},{10,58},{12,60},{14,62},{16,32}... | collective-permute-start | bytes 786440 | tf_op jit(solution)/shard_map/ppermute | solution.py:354
  60.0 8.2 %collective-permute-start.15 = (bf16[4,2,128,128]{3,2,1,0:T(8,128)(2,1)S(1)}, bf16[4,2,128,128]{3,2,1,0:T(8,128)(2,1)S(1)}, u32[]{:S(2)}, u32[]{:S(2)}) collective-permute-start(bf16[4,2,128,128]{3,2,1,0:T(8,128)(2,1)S(1)} %pad_maximum_fusion.4.refs_1_), channel_id=1, source_target_pairs={{0,14},{2,4},{4,2},{6,8},{8,6},{10,12},{12,10},{14,0},{16,30},{18,... | collective-permute-start | bytes 786440 | tf_op jit(solution)/shard_map/ppermute | solution.py:306
  61.8 8.6 %collective-permute-start.16 = (bf16[4,2,128,128]{3,2,1,0:T(8,128)(2,1)S(1)}, bf16[4,2,128,128]{3,2,1,0:T(8,128)(2,1)S(1)}, u32[]{:S(2)}, u32[]{:S(2)}) collective-permute-start(bf16[4,2,128,128]{3,2,1,0:T(8,128)(2,1)S(1)} %pad_maximum_fusion.3.refs_0_), channel_id=1, source_target_pairs={{0,2},{2,0},{4,6},{6,4},{8,10},{10,8},{12,14},{14,12},{16,18},{18,... | collective-permute-start | bytes 786440 | tf_op jit(solution)/shard_map/ppermute | solution.py:302
  68.3 8.1 %collective-permute-start.18 = (bf16[4,2,128,128]{3,2,1,0:T(8,128)(2,1)S(1)}, bf16[4,2,128,128]{3,2,1,0:T(8,128)(2,1)S(1)}, u32[]{:S(2)}, u32[]{:S(2)}) collective-permute-start(bf16[4,2,128,128]{3,2,1,0:T(8,128)(2,1)S(1)} %add_convert_fusion.3.refs_0_), channel_id=1, source_target_pairs={{0,2},{2,0},{4,6},{6,4},{8,10},{10,8},{12,14},{14,12},{16,18},{18,... | collective-permute-start | bytes 786440 | tf_op jit(solution)/shard_map/ppermute | solution.py:302
  70.5 9.0 %collective-permute-start.17 = (bf16[4,2,128,128]{3,2,1,0:T(8,128)(2,1)S(1)}, bf16[4,2,128,128]{3,2,1,0:T(8,128)(2,1)S(1)}, u32[]{:S(2)}, u32[]{:S(2)}) collective-permute-start(bf16[4,2,128,128]{3,2,1,0:T(8,128)(2,1)S(1)} %add_convert_fusion.2.refs_1_), channel_id=1, source_target_pairs={{0,14},{2,4},{4,2},{6,8},{8,6},{10,12},{12,10},{14,0},{16,30},{18,... | collective-permute-start | bytes 786440 | tf_op jit(solution)/shard_map/ppermute | solution.py:306
  76.5 9.9 %collective-permute-start.22 = (bf16[4,2,128,128]{3,2,1,0:T(8,128)(2,1)S(1)}, bf16[4,2,128,128]{3,2,1,0:T(8,128)(2,1)S(1)}, u32[]{:S(2)}, u32[]{:S(2)}) collective-permute-start(bf16[4,2,128,128]{3,2,1,0:T(8,128)(2,1)S(1)} %add_convert_fusion.refs_1_), channel_id=1, source_target_pairs={{0,14},{2,4},{4,2},{6,8},{8,6},{10,12},{12,10},{14,0},{16,30},{18,... | collective-permute-start | bytes 786440 | tf_op jit(solution)/shard_map/ppermute | solution.py:306
  79.6 6.8 %collective-permute-start.21 = (bf16[4,2,128,128]{3,2,1,0:T(8,128)(2,1)S(1)}, bf16[4,2,128,128]{3,2,1,0:T(8,128)(2,1)S(1)}, u32[]{:S(2)}, u32[]{:S(2)}) collective-permute-start(bf16[4,2,128,128]{3,2,1,0:T(8,128)(2,1)S(1)} %add_convert_fusion.1.refs_0_), channel_id=1, source_target_pairs={{0,2},{2,0},{4,6},{6,4},{8,10},{10,8},{12,14},{14,12},{16,18},{18,... | collective-permute-start | bytes 786440 | tf_op jit(solution)/shard_map/ppermute | solution.py:302
  84.9 7.7 %collective-permute-start.20 = (bf16[1024,128]{1,0:T(8,128)(2,1)S(1)}, bf16[1024,128]{1,0:T(8,128)(2,1)S(1)}, u32[]{:S(2)}, u32[]{:S(2)}) collective-permute-start(bf16[1024,128]{1,0:T(8,128)(2,1)S(1)} %get-tuple-element.68), channel_id=1, source_target_pairs={{0,48},{2,50},{4,52},{6,54},{8,56},{10,58},{12,60},{14,62},{16,32}... | collective-permute-start | bytes 786440 | tf_op jit(solution)/shard_map/ppermute | solution.py:371
  86.5 7.0 %collective-permute-start.23 = (bf16[2,128,128]{2,1,0:T(8,128)(2,1)S(1)}, bf16[2,128,128]{2,1,0:T(8,128)(2,1)S(1)}, u32[]{:S(2)}, u32[]{:S(2)}) collective-permute-start(bf16[2,128,128]{2,1,0:T(8,128)(2,1)S(1)} %get-tuple-element.88), channel_id=1, source_target_pairs={{0,16},{2,18},{4,20},{6,22},{8,24},{10,26},{12,28},{14,30},{16,0},... | collective-permute-start | bytes 196616 | tf_op jit(solution)/shard_map/ppermute | solution.py:380
  89.2 5.5 %collective-permute-start.25 = (bf16[2,128,128]{2,1,0:T(8,128)(2,1)S(1)}, bf16[2,128,128]{2,1,0:T(8,128)(2,1)S(1)}, u32[]{:S(2)}, u32[]{:S(2)}) collective-permute-start(bf16[2,128,128]{2,1,0:T(8,128)(2,1)S(1)} %get-tuple-element.89), channel_id=1, source_target_pairs={{0,48},{2,50},{4,52},{6,54},{8,56},{10,58},{12,60},{14,62},{16,32}... | collective-permute-start | bytes 196616 | tf_op jit(solution)/shard_map/ppermute | solution.py:380
  91.2 5.8 %collective-permute-start.24 = (bf16[2,128,128]{2,1,0:T(8,128)(2,1)S(1)}, bf16[2,128,128]{2,1,0:T(8,128)(2,1)S(1)}, u32[]{:S(2)}, u32[]{:S(2)}) collective-permute-start(bf16[2,128,128]{2,1,0:T(8,128)(2,1)S(1)} %get-tuple-element.90), channel_id=1, source_target_pairs={{0,32},{2,34},{4,36},{6,38},{8,40},{10,42},{12,44},{14,46},{16,48}... | collective-permute-start | bytes 196616 | tf_op jit(solution)/shard_map/ppermute | solution.py:380
  (7 other events, 19.0 us)
where the time goes:
time: 100 us; the launch traced here: 98.5 us
  starting transfers between devices  38.9 us (39%)
  Pallas kernels  33 us (33%)
  waiting for transfers between devices  19 us (19%)
  local copies, waits for them, and re-layouts  3.84 us (4%)
  other arithmetic  2.75 us (3%)
    pallas_call x9, Pallas kernels, run_stage(): pl.pallas_call(functools.partial(stage_kernel, stage, len(after), len(pas...  33 us
    ppermute x8, starting transfers between devices, swap_odd(): return lax.ppermute(array, 'ctx', swap_z(1))  13.7 us
    ppermute x8, starting transfers between devices, swap_even(): return lax.ppermute(array, 'ctx', swap_z(0))  10.5 us
    ppermute x8, waiting for transfers between devices, swap_odd(): return lax.ppermute(array, 'ctx', swap_z(1))  6.18 us
    ppermute x8, waiting for transfers between devices, swap_even(): return lax.ppermute(array, 'ctx', swap_z(0))  5.7 us
    ppermute x3, starting transfers between devices, on_device(): lax.ppermute(sums[slot].astype(jnp.bfloat16), 'ctx', swap_y(mask))  4.86 us
    ppermute x3, starting transfers between devices, on_device(): lax.ppermute(pairs[mask // 2], 'ctx', swap_y(mask))  4.43 us
    unnamed x12, local copies, waits for them, and re-layouts  3.59 us
  transfers between devices with their start and end apart: 26, of which 14 were waited for; matrix products, arithmetic and copies ran while one was open for 3% of the time, Pallas kernels for 29%

commit v1 on v0

--- a/solution.py
+++ b/solution.py
@@ -99,26 +99,29 @@
     def part_facts(part):
         query_block = jnp.where(part == 0, y, NY - 1 - y) * NZ + z
         first_pos = query_block * block
-        return query_block, doc_start(first_pos), doc_start(first_pos + block - 1)
+        positions = first_pos + lax.broadcasted_iota(jnp.int32, (1, lanes), 1) // group
+        ends = doc_start(first_pos), doc_start(first_pos + block - 1)
+        return query_block, *ends, positions, doc_start(positions)
 
     def is_live(unit, facts):
-        query_block, open_first, _ = facts
+        query_block, open_first = facts[:2]
         return [(n <= query_block) & ((n + 1) * block > open_first) for n in blocks_of(unit)]
 
     def is_clear(unit, facts):
-        query_block, _, open_last = facts
+        query_block, open_last = facts[0], facts[2]
         one, two = ((n < query_block) & (n * block >= open_last) for n in blocks_of(unit))
         return one & two
 
     def scores_of(unit, rows, part, facts, masked):
         scores = dot_nt(k_scr[unit, rows, :], q_scr[part])
         if masked:
-            lane = lax.broadcasted_iota(jnp.int32, (1, lanes), 1)
-            positions = facts[0] * block + lane // group
             one, two = blocks_of(unit)
             row = lax.broadcasted_iota(jnp.int32, scores.shape, 0)
-            key_pos = row + jnp.where(rows.start == 0, one, two) * block
-            allowed = (key_pos <= positions) & (key_pos >= doc_start(positions))
+            if scores.shape[0] == block:
+                key_pos = row + jnp.where(rows.start == 0, one, two) * block
+            else:
+                key_pos = row + jnp.where(row < block, one, two - 1) * block
+            allowed = (key_pos <= facts[3]) & (key_pos >= facts[4])
             scores = jnp.where(allowed, scores, MASKED_SCORE)
         return scores
 
@@ -126,15 +129,21 @@
         def step(unit, _):
             one, two = is_live(unit, facts)
             clear = is_clear(unit, facts) & one & two
-            pl.when(clear)(lambda: work(unit, pl.ds(0, 2 * block), False))
-
-            def half_step(half, _):
-                live = jnp.where(half == 0, one, two) & jnp.logical_not(clear)
-                rows = pl.ds(pl.multiple_of(half * block, block), block)
-                pl.when(live)(lambda: work(unit, rows, True))
+            whole = pl.ds(0, 2 * block)
+            pl.when(clear)(lambda: work(unit, whole, False))
+            if kind == "own":
+
+                def half_step(half, _):
+                    live = jnp.where(half == 0, one, two) & jnp.logical_not(clear)
+                    rows = pl.ds(pl.multiple_of(half * block, block), block)
+                    pl.when(live)(lambda: work(unit, rows, True))
+                    return 0
+
+                lax.fori_loop(0, 2, half_step, 0)
                 return 0
-
-            lax.fori_loop(0, 2, half_step, 0)
+            pl.when(one & two & jnp.logical_not(clear))(lambda: work(unit, whole, True))
+            half = pl.ds(pl.multiple_of(jnp.where(one, 0, block), block), block)
+            pl.when(one ^ two)(lambda: work(unit, half, True))
             return 0
 
         lax.fori_loop(0, units, step, 0)

time: 100 us -> 100 us (level); the launches traced: 98.5 us -> 99.8 us
  waiting for transfers between devices: 19 us -> 21.4 us
  Pallas kernels: 33 us -> 31.8 us
    ppermute x8, starting transfers between devices: 13.7 us -> 20.2 us  [swap_odd(): return lax.ppermute(array, 'ctx', swap_z(1))]
    ppermute x8, starting transfers between devices: 10.5 us -> 4.56 us  [swap_even(): return lax.ppermute(array, 'ctx', swap_z(0))]
    ppermute x8, waiting for transfers between devices: 6.18 us -> 7.8 us  [swap_odd(): return lax.ppermute(array, 'ctx', swap_z(1))]
    ppermute x8, waiting for transfers between devices: 5.7 us -> 7.07 us  [swap_even(): return lax.ppermute(array, 'ctx', swap_z(0))]
    pallas_call x9, Pallas kernels: 33 us -> 31.8 us  [run_stage(): pl.pallas_call(functools.partial(stage_kernel, stage, len(after), len(pas...]
  transfers between devices with their start and end apart: 26 -> 26, of which waited for: 14 -> 15; matrix products, arithmetic and copies ran while one was open for 3% -> 3% of each run, Pallas kernels for 29% -> 27%
where the time goes in v1:
time: 100 us; the launch traced here: 99.8 us
  starting transfers between devices  39 us (39%)
  Pallas kernels  31.8 us (32%)
  waiting for transfers between devices  21.4 us (21%)
  local copies, waits for them, and re-layouts  3.84 us (4%)
  other arithmetic  2.75 us (3%)
  between operations  1.02 us (1%)
    pallas_call x9, Pallas kernels, run_stage(): pl.pallas_call(functools.partial(stage_kernel, stage, len(after), len(pas...  31.8 us
    ppermute x8, starting transfers between devices, swap_odd(): return lax.ppermute(array, 'ctx', swap_z(1))  20.2 us
    ppermute x8, waiting for transfers between devices, swap_odd(): return lax.ppermute(array, 'ctx', swap_z(1))  7.8 us
    ppermute x8, waiting for transfers between devices, swap_even(): return lax.ppermute(array, 'ctx', swap_z(0))  7.07 us
    ppermute x8, starting transfers between devices, swap_even(): return lax.ppermute(array, 'ctx', swap_z(0))  4.56 us
    ppermute x3, starting transfers between devices, on_device(): lax.ppermute(pairs[mask // 2], 'ctx', swap_y(mask))  4.43 us
    ppermute x3, starting transfers between devices, on_device(): lax.ppermute(sums[slot].astype(jnp.bfloat16), 'ctx', swap_y(mask))  4.18 us
    unnamed x12, local copies, waits for them, and re-layouts  3.59 us
  transfers between devices with their start and end apart: 26, of which 15 were waited for; matrix products, arithmetic and copies ran while one was open for 3% of the time, Pallas kernels for 27%

profile of v1, /device:TPU:6, one launch (start us, length us, event | category | flops | bytes accessed | tf_op | source)
XLA Modules:
  0.0 99.8 jit_solution(8987081928803487551)
XLA Ops:
  2.5 3.3 %collective-permute-start.3 = (bf16[2,128,128]{2,1,0:T(8,128)(2,1)S(1)}, bf16[2,128,128]{2,1,0:T(8,128)(2,1)S(1)}, u32[]{:S(2)}, u32[]{:S(2)}) collective-permute-start(bf16[2,128,128]{2,1,0:T(8,128)(2,1)S(1)} %pad_maximum_fusion.7), channel_id=1, source_target_pairs={{0,32},{2,34},{4,36},{6,38},{8,40},{10,42},{12,44},{14,46},{16,48}... | collective-permute-start | bytes 196616 | tf_op jit(solution)/shard_map/ppermute | solution.py:334
  7.0 2.3 %collective-permute-start = (bf16[1024,128]{1,0:T(8,128)(2,1)S(1)}, bf16[1024,128]{1,0:T(8,128)(2,1)S(1)}, u32[]{:S(2)}, u32[]{:S(2)}) collective-permute-start(bf16[1024,128]{1,0:T(8,128)(2,1)S(1)} %get-tuple-element.86), channel_id=1, source_target_pairs={{0,48},{2,50},{4,52},{6,54},{8,56},{10,58},{12,60},{14,62},{16,32}... | collective-permute-start | bytes 786440 | tf_op jit(solution)/shard_map/ppermute | solution.py:337
  11.9 2.0 %collective-permute-start.9 = (bf16[4,2,128,128]{3,2,1,0:T(8,128)(2,1)S(1)}, bf16[4,2,128,128]{3,2,1,0:T(8,128)(2,1)S(1)}, u32[]{:S(2)}, u32[]{:S(2)}) collective-permute-start(bf16[4,2,128,128]{3,2,1,0:T(8,128)(2,1)S(1)} %pad_maximum_fusion.2.refs_4_.refs_8_), channel_id=1, source_target_pairs={{0,2},{2,0},{4,6},{6,4},{8,10},{10,8},{12,14},{14,12},{16,18},{18,... | collective-permute-start | bytes 786440 | tf_op jit(solution)/shard_map/ppermute | solution.py:311
  13.9 4.9 %collective-permute-start.5 = (bf16[4,2,128,128]{3,2,1,0:T(8,128)(2,1)S(1)}, bf16[4,2,128,128]{3,2,1,0:T(8,128)(2,1)S(1)}, u32[]{:S(2)}, u32[]{:S(2)}) collective-permute-start(bf16[4,2,128,128]{3,2,1,0:T(8,128)(2,1)S(1)} %pad_maximum_fusion.2.refs_4_.refs_8_), channel_id=1, source_target_pairs={{0,14},{2,4},{4,2},{6,8},{8,6},{10,12},{12,10},{14,0},{16,30},{18,... | collective-permute-start | bytes 786440 | tf_op jit(solution)/shard_map/ppermute | solution.py:315
  19.6 3.0 %fwdown.1 = (f32[2,8,1024]{2,1,0:T(8,128)S(1)}, f32[2,8,1024]{2,1,0:T(8,128)S(1)}, f32[2,128,1024]{2,1,0:T(8,128)S(1)}, bf16[1024,128]{1,0:T(8,128)(2,1)S(1)}) custom-call(s32[16]{0:T(128)S(1)} %copy-done, s32[3]{0:T(128)S(1)} %get-tuple-element.105.refs_1_.refs_3_, ...), custom_call_target="tpu_custom_call", output_to_operand_aliasing={{3}: (5, {})} | custom-call | flops 1610612736 | bytes 4194304 | tf_op jit(solution)/shard_map/fwdown/pallas_call | solution.py:277
  24.1 2.4 %collective-permute-start.10 = (bf16[4,2,128,128]{3,2,1,0:T(8,128)(2,1)S(1)}, bf16[4,2,128,128]{3,2,1,0:T(8,128)(2,1)S(1)}, u32[]{:S(2)}, u32[]{:S(2)}) collective-permute-start(bf16[4,2,128,128]{3,2,1,0:T(8,128)(2,1)S(1)} %collective-permute-done.9.refs_4_.refs_8_), channel_id=1, source_target_pairs={{0,14},{2,4},{4,2},{6,8},{8,6},{10,12},{12,10},{14,0},{16,30},{18,... | collective-permute-start | bytes 786440 | tf_op jit(solution)/shard_map/ppermute | solution.py:315
  26.5 3.2 %fwdpair.3 = (f32[2,8,1024]{2,1,0:T(8,128)S(1)}, f32[2,8,1024]{2,1,0:T(8,128)S(1)}, f32[2,128,1024]{2,1,0:T(8,128)S(1)}) custom-call(s32[16]{0:T(128)S(1)} %copy-done, s32[3]{0:T(128)S(1)} %get-tuple-element.76.refs_1_.refs_3_, bf16[1024,128]{1,0:T(8,128)(2,1)S(1)} %get-tuple-element.87.refs_2_.refs_4_, ...), custom_call_target="tpu_custom_call", output_to_operand_aliasing={{0}: (6, {}), {1}: (7, {}), {2}: (8, {})} | custom-call | flops 3221225472 | bytes 4194304 | tf_op jit(solution)/shard_map/fwdpair/pallas_call | solution.py:277
  29.7 2.0 %collective-permute-done.10.refs_5_.refs_9_ = bf16[4,2,128,128]{3,2,1,0:T(8,128)(2,1)S(1)} collective-permute-done((bf16[4,2,128,128]{3,2,1,0:T(8,128)(2,1)S(1)}, bf16[4,2,128,128]{3,2,1,0:T(8,128)(2,1)S(1)}, u32[]{:S(2)}, u32[]{:S(2)}) %collective-permute-start.10) | collective-permute-done | bytes 262176 | tf_op jit(solution)/shard_map/ppermute | solution.py:315
  32.8 1.9 %collective-permute-done.6.refs_4_.refs_8_ = bf16[4,2,128,128]{3,2,1,0:T(8,128)(2,1)S(1)} collective-permute-done((bf16[4,2,128,128]{3,2,1,0:T(8,128)(2,1)S(1)}, bf16[4,2,128,128]{3,2,1,0:T(8,128)(2,1)S(1)}, u32[]{:S(2)}, u32[]{:S(2)}) %collective-permute-start.6) | collective-permute-done | bytes 262176 | tf_op jit(solution)/shard_map/ppermute | solution.py:311
  34.7 3.1 %fwdpair.4 = (f32[2,8,1024]{2,1,0:T(8,128)S(1)}, f32[2,8,1024]{2,1,0:T(8,128)S(1)}, f32[2,128,1024]{2,1,0:T(8,128)S(1)}) custom-call(s32[16]{0:T(128)S(1)} %copy-done, s32[3]{0:T(128)S(1)} %get-tuple-element.103.refs_1_.refs_3_, bf16[1024,128]{1,0:T(8,128)(2,1)S(1)} %get-tuple-element.87.refs_2_.refs_4_, ...), custom_call_target="tpu_custom_call", output_to_operand_aliasing={{0}: (6, {}), {1}: (7, {}), {2}: (8, {})} | custom-call | flops 3221225472 | bytes 4194304 | tf_op jit(solution)/shard_map/fwdpair/pallas_call | solution.py:277
  38.5 2.0 %collective-permute-start.12 = (bf16[2,2,128,128]{3,2,1,0:T(8,128)(2,1)S(1)}, bf16[2,2,128,128]{3,2,1,0:T(8,128)(2,1)S(1)}, u32[]{:S(2)}, u32[]{:S(2)}) collective-permute-start(bf16[2,2,128,128]{3,2,1,0:T(8,128)(2,1)S(1)} %slice.92), channel_id=1, source_target_pairs={{0,14},{2,4},{4,2},{6,8},{8,6},{10,12},{12,10},{14,0},{16,30},{18,... | collective-permute-start | bytes 393224 | tf_op jit(solution)/shard_map/ppermute | solution.py:315
  40.6 3.1 %collective-permute-done.7.refs_5_.refs_7_ = bf16[4,2,128,128]{3,2,1,0:T(8,128)(2,1)S(1)} collective-permute-done((bf16[4,2,128,128]{3,2,1,0:T(8,128)(2,1)S(1)}, bf16[4,2,128,128]{3,2,1,0:T(8,128)(2,1)S(1)}, u32[]{:S(2)}, u32[]{:S(2)}) %collective-permute-start.7) | collective-permute-done | bytes 262176 | tf_op jit(solution)/shard_map/ppermute | solution.py:315
  44.0 3.1 %fwdpair.5 = (f32[2,8,1024]{2,1,0:T(8,128)S(1)}, f32[2,8,1024]{2,1,0:T(8,128)S(1)}, f32[2,128,1024]{2,1,0:T(8,128)S(1)}) custom-call(s32[16]{0:T(128)S(1)} %copy-done, s32[3]{0:T(128)S(1)} %get-tuple-element.104.refs_1_, bf16[1024,128]{1,0:T(8,128)(2,1)S(1)} %get-tuple-element.87.refs_2_.refs_4_, ...), custom_call_target="tpu_custom_call", output_to_operand_aliasing={{0}: (6, {}), {1}: (7, {}), {2}: (8, {})} | custom-call | flops 3221225472 | bytes 4194304 | tf_op jit(solution)/shard_map/fwdpair/pallas_call | solution.py:277
  48.9 4.6 %fwdbwdfar.1 = (bf16[1024,128]{1,0:T(8,128)(2,1)S(1)}, bf16[1024,128]{1,0:T(8,128)(2,1)S(1)}, f32[2,8,1024]{2,1,0:T(8,128)S(1)}, f32[2,8,1024]{2,1,0:T(8,128)S(1...) custom-call(s32[16]{0:T(128)S(1)} %copy-done, ...), custom_call_target="tpu_custom_call" | custom-call | flops 5637144576 | bytes 4194304 | tf_op jit(solution)/shard_map/fwdbwdfar/pallas_call | solution.py:277
  56.0 3.6 %bwdpair.3 = (f32[2,128,1024]{2,1,0:T(8,128)S(1)}, bf16[4,2,128,128]{3,2,1,0:T(8,128)(2,1)S(1)}, bf16[4,2,128,128]{3,2,1,0:T(8,128)(2,1)S(1)}) custom-call(s32[16]{0:T(128)S(1)} %copy-done, s32[3]{0:T(128)S(1)} %get-tuple-element.104.refs_1_, bf16[1024,128]{1,0:T(8,128)(2,1)S(1)} %get-tuple-element.87.refs_2_.refs_4_, ...), custom_call_target="tpu_custom_call", output_to_operand_aliasing={{0}: (10, {})} | custom-call | flops 8053063680 | bytes 4194304 | tf_op jit(solution)/shard_map/bwdpair/pallas_call | solution.py:277
  59.8 3.5 %collective-permute-start.15 = (bf16[4,2,128,128]{3,2,1,0:T(8,128)(2,1)S(1)}, bf16[4,2,128,128]{3,2,1,0:T(8,128)(2,1)S(1)}, u32[]{:S(2)}, u32[]{:S(2)}) collective-permute-start(bf16[4,2,128,128]{3,2,1,0:T(8,128)(2,1)S(1)} %pad_maximum_fusion.4.refs_1_), channel_id=1, source_target_pairs={{0,14},{2,4},{4,2},{6,8},{8,6},{10,12},{12,10},{14,0},{16,30},{18,... | collective-permute-start | bytes 786440 | tf_op jit(solution)/shard_map/ppermute | solution.py:315
  63.8 3.6 %bwdpair.4 = (f32[2,128,1024]{2,1,0:T(8,128)S(1)}, bf16[4,2,128,128]{3,2,1,0:T(8,128)(2,1)S(1)}, bf16[4,2,128,128]{3,2,1,0:T(8,128)(2,1)S(1)}) custom-call(bf16[4,2,128,128]{3,2,1,0:T(8,128)(2,1)S(1)} %pad_maximum_fusion.3.refs_0_, bf16[4,2,128,128]{3,2,1,0:T(8,128)(2,1)S(1)} %pad_maximum_fusion.4.refs_1_, ...), custom_call_target="tpu_custom_call", output_to_operand_aliasing={{0}: (12, {})} | custom-call | flops 8053063680 | bytes 4194304 | tf_op jit(solution)/shard_map/bwdpair/pallas_call | solution.py:277
  67.4 2.7 %collective-permute-done.15 = bf16[4,2,128,128]{3,2,1,0:T(8,128)(2,1)S(1)} collective-permute-done((bf16[4,2,128,128]{3,2,1,0:T(8,128)(2,1)S(1)}, bf16[4,2,128,128]{3,2,1,0:T(8,128)(2,1)S(1)}, u32[]{:S(2)}, u32[]{:S(2)}) %collective-permute-start.15) | collective-permute-done | bytes 262176 | tf_op jit(solution)/shard_map/ppermute | solution.py:315
  70.4 3.6 %collective-permute-start.17 = (bf16[4,2,128,128]{3,2,1,0:T(8,128)(2,1)S(1)}, bf16[4,2,128,128]{3,2,1,0:T(8,128)(2,1)S(1)}, u32[]{:S(2)}, u32[]{:S(2)}) collective-permute-start(bf16[4,2,128,128]{3,2,1,0:T(8,128)(2,1)S(1)} %add_convert_fusion.2.refs_1_), channel_id=1, source_target_pairs={{0,14},{2,4},{4,2},{6,8},{8,6},{10,12},{12,10},{14,0},{16,30},{18,... | collective-permute-start | bytes 786440 | tf_op jit(solution)/shard_map/ppermute | solution.py:315
  74.1 3.8 %bwdpair.5 = (f32[2,128,1024]{2,1,0:T(8,128)S(1)}, bf16[4,2,128,128]{3,2,1,0:T(8,128)(2,1)S(1)}, bf16[4,2,128,128]{3,2,1,0:T(8,128)(2,1)S(1)}) custom-call(bf16[4,2,128,128]{3,2,1,0:T(8,128)(2,1)S(1)} %add_convert_fusion.3.refs_0_, bf16[4,2,128,128]{3,2,1,0:T(8,128)(2,1)S(1)} %add_convert_fusion.2.refs_1_, ...), custom_call_target="tpu_custom_call", output_to_operand_aliasing={{0}: (12, {})} | custom-call | flops 8053063680 | bytes 4194304 | tf_op jit(solution)/shard_map/bwdpair/pallas_call | solution.py:277
  78.8 3.6 %collective-permute-start.22 = (bf16[4,2,128,128]{3,2,1,0:T(8,128)(2,1)S(1)}, bf16[4,2,128,128]{3,2,1,0:T(8,128)(2,1)S(1)}, u32[]{:S(2)}, u32[]{:S(2)}) collective-permute-start(bf16[4,2,128,128]{3,2,1,0:T(8,128)(2,1)S(1)} %add_convert_fusion.refs_1_), channel_id=1, source_target_pairs={{0,14},{2,4},{4,2},{6,8},{8,6},{10,12},{12,10},{14,0},{16,30},{18,... | collective-permute-start | bytes 786440 | tf_op jit(solution)/shard_map/ppermute | solution.py:315
  82.5 3.7 %bwdown.1 = (bf16[1024,128]{1,0:T(8,128)(2,1)S(1)}, bf16[1024,128]{1,0:T(8,128)(2,1)S(1)}, bf16[4,2,128,128]{3,2,1,0:T(8,128)(2,1)S(1)}, bf16[1024,128]{1,0:T(8,128)(2,1)S(1)}) custom-call(bf16[4,2,128,128]{3,2,1,0:T(8,128)(2,1)S(1)} %add_convert_fusion.1.refs_0_, ...), custom_call_target="tpu_custom_call", output_to_operand_aliasing={{3}: (12, {})} | custom-call | flops 4026531840 | bytes 4194304 | tf_op jit(solution)/shard_map/bwdown/pallas_call | solution.py:277
  89.7 2.8 %collective-permute-start.25 = (bf16[2,128,128]{2,1,0:T(8,128)(2,1)S(1)}, bf16[2,128,128]{2,1,0:T(8,128)(2,1)S(1)}, u32[]{:S(2)}, u32[]{:S(2)}) collective-permute-start(bf16[2,128,128]{2,1,0:T(8,128)(2,1)S(1)} %get-tuple-element.89), channel_id=1, source_target_pairs={{0,48},{2,50},{4,52},{6,54},{8,56},{10,58},{12,60},{14,62},{16,32}... | collective-permute-start | bytes 196616 | tf_op jit(solution)/shard_map/ppermute | solution.py:389
  95.2 3.1 %collective-permute-done.24 = bf16[2,128,128]{2,1,0:T(8,128)(2,1)S(1)} collective-permute-done((bf16[2,128,128]{2,1,0:T(8,128)(2,1)S(1)}, bf16[2,128,128]{2,1,0:T(8,128)(2,1)S(1)}, u32[]{:S(2)}, u32[]{:S(2)}) %collective-permute-start.24) | collective-permute-done | bytes 65568 | tf_op jit(solution)/shard_map/ppermute | solution.py:389
  (79 shorter events, 23.7 us)
Async XLA Ops:
  2.5 8.7 %collective-permute-start.3 = (bf16[2,128,128]{2,1,0:T(8,128)(2,1)S(1)}, bf16[2,128,128]{2,1,0:T(8,128)(2,1)S(1)}, u32[]{:S(2)}, u32[]{:S(2)}) collective-permute-start(bf16[2,128,128]{2,1,0:T(8,128)(2,1)S(1)} %pad_maximum_fusion.7), channel_id=1, source_target_pairs={{0,32},{2,34},{4,36},{6,38},{8,40},{10,42},{12,44},{14,46},{16,48}... | collective-permute-start | bytes 196616 | tf_op jit(solution)/shard_map/ppermute | solution.py:334
  5.7 6.1 %collective-permute-start.2 = (bf16[2,128,128]{2,1,0:T(8,128)(2,1)S(1)}, bf16[2,128,128]{2,1,0:T(8,128)(2,1)S(1)}, u32[]{:S(2)}, u32[]{:S(2)}) collective-permute-start(bf16[2,128,128]{2,1,0:T(8,128)(2,1)S(1)} %pad_maximum_fusion.7), channel_id=1, source_target_pairs={{0,48},{2,50},{4,52},{6,54},{8,56},{10,58},{12,60},{14,62},{16,32}... | collective-permute-start | bytes 196616 | tf_op jit(solution)/shard_map/ppermute | solution.py:334
  7.0 11.9 %collective-permute-start = (bf16[1024,128]{1,0:T(8,128)(2,1)S(1)}, bf16[1024,128]{1,0:T(8,128)(2,1)S(1)}, u32[]{:S(2)}, u32[]{:S(2)}) collective-permute-start(bf16[1024,128]{1,0:T(8,128)(2,1)S(1)} %get-tuple-element.86), channel_id=1, source_target_pairs={{0,48},{2,50},{4,52},{6,54},{8,56},{10,58},{12,60},{14,62},{16,32}... | collective-permute-start | bytes 786440 | tf_op jit(solution)/shard_map/ppermute | solution.py:337
  11.9 12.3 %collective-permute-start.9 = (bf16[4,2,128,128]{3,2,1,0:T(8,128)(2,1)S(1)}, bf16[4,2,128,128]{3,2,1,0:T(8,128)(2,1)S(1)}, u32[]{:S(2)}, u32[]{:S(2)}) collective-permute-start(bf16[4,2,128,128]{3,2,1,0:T(8,128)(2,1)S(1)} %pad_maximum_fusion.2.refs_4_.refs_8_), channel_id=1, source_target_pairs={{0,2},{2,0},{4,6},{6,4},{8,10},{10,8},{12,14},{14,12},{16,18},{18,... | collective-permute-start | bytes 786440 | tf_op jit(solution)/shard_map/ppermute | solution.py:311
  13.9 12.6 %collective-permute-start.5 = (bf16[4,2,128,128]{3,2,1,0:T(8,128)(2,1)S(1)}, bf16[4,2,128,128]{3,2,1,0:T(8,128)(2,1)S(1)}, u32[]{:S(2)}, u32[]{:S(2)}) collective-permute-start(bf16[4,2,128,128]{3,2,1,0:T(8,128)(2,1)S(1)} %pad_maximum_fusion.2.refs_4_.refs_8_), channel_id=1, source_target_pairs={{0,14},{2,4},{4,2},{6,8},{8,6},{10,12},{12,10},{14,0},{16,30},{18,... | collective-permute-start | bytes 786440 | tf_op jit(solution)/shard_map/ppermute | solution.py:315
  22.5 24.6 %collective-permute-start.4 = (bf16[1024,128]{1,0:T(8,128)(2,1)S(1)}, bf16[1024,128]{1,0:T(8,128)(2,1)S(1)}, u32[]{:S(2)}, u32[]{:S(2)}) collective-permute-start(bf16[1024,128]{1,0:T(8,128)(2,1)S(1)} %get-tuple-element.37), channel_id=1, source_target_pairs={{0,48},{2,50},{4,52},{6,54},{8,56},{10,58},{12,60},{14,62},{16,32}... | collective-permute-start | bytes 786440 | tf_op jit(solution)/shard_map/ppermute | solution.py:356
  24.1 7.6 %collective-permute-start.10 = (bf16[4,2,128,128]{3,2,1,0:T(8,128)(2,1)S(1)}, bf16[4,2,128,128]{3,2,1,0:T(8,128)(2,1)S(1)}, u32[]{:S(2)}, u32[]{:S(2)}) collective-permute-start(bf16[4,2,128,128]{3,2,1,0:T(8,128)(2,1)S(1)} %collective-permute-done.9.refs_4_.refs_8_), channel_id=1, source_target_pairs={{0,14},{2,4},{4,2},{6,8},{8,6},{10,12},{12,10},{14,0},{16,30},{18,... | collective-permute-start | bytes 786440 | tf_op jit(solution)/shard_map/ppermute | solution.py:315
  26.5 8.2 %collective-permute-start.6 = (bf16[4,2,128,128]{3,2,1,0:T(8,128)(2,1)S(1)}, bf16[4,2,128,128]{3,2,1,0:T(8,128)(2,1)S(1)}, u32[]{:S(2)}, u32[]{:S(2)}) collective-permute-start(bf16[4,2,128,128]{3,2,1,0:T(8,128)(2,1)S(1)} %collective-permute-done.5.refs_5_.refs_9_), channel_id=1, source_target_pairs={{0,2},{2,0},{4,6},{6,4},{8,10},{10,8},{12,14},{14,12},{16,18},{18,... | collective-permute-start | bytes 786440 | tf_op jit(solution)/shard_map/ppermute | solution.py:311
  31.7 6.8 %collective-permute-start.11 = (bf16[4,2,128,128]{3,2,1,0:T(8,128)(2,1)S(1)}, bf16[4,2,128,128]{3,2,1,0:T(8,128)(2,1)S(1)}, u32[]{:S(2)}, u32[]{:S(2)}) collective-permute-start(bf16[4,2,128,128]{3,2,1,0:T(8,128)(2,1)S(1)} %collective-permute-done.10.refs_5_.refs_9_), channel_id=1, source_target_pairs={{0,2},{2,0},{4,6},{6,4},{8,10},{10,8},{12,14},{14,12},{16,18},{18,... | collective-permute-start | bytes 786440 | tf_op jit(solution)/shard_map/ppermute | solution.py:311
  34.7 9.0 %collective-permute-start.7 = (bf16[4,2,128,128]{3,2,1,0:T(8,128)(2,1)S(1)}, bf16[4,2,128,128]{3,2,1,0:T(8,128)(2,1)S(1)}, u32[]{:S(2)}, u32[]{:S(2)}) collective-permute-start(bf16[4,2,128,128]{3,2,1,0:T(8,128)(2,1)S(1)} %collective-permute-done.6.refs_4_.refs_8_), channel_id=1, source_target_pairs={{0,14},{2,4},{4,2},{6,8},{8,6},{10,12},{12,10},{14,0},{16,30},{18,... | collective-permute-start | bytes 786440 | tf_op jit(solution)/shard_map/ppermute | solution.py:315
  38.5 8.6 %collective-permute-start.12 = (bf16[2,2,128,128]{3,2,1,0:T(8,128)(2,1)S(1)}, bf16[2,2,128,128]{3,2,1,0:T(8,128)(2,1)S(1)}, u32[]{:S(2)}, u32[]{:S(2)}) collective-permute-start(bf16[2,2,128,128]{3,2,1,0:T(8,128)(2,1)S(1)} %slice.92), channel_id=1, source_target_pairs={{0,14},{2,4},{4,2},{6,8},{8,6},{10,12},{12,10},{14,0},{16,30},{18,... | collective-permute-start | bytes 393224 | tf_op jit(solution)/shard_map/ppermute | solution.py:315
  53.5 9.8 %collective-permute-start.13 = (bf16[2,2,128,128]{3,2,1,0:T(8,128)(2,1)S(1)}, bf16[2,2,128,128]{3,2,1,0:T(8,128)(2,1)S(1)}, u32[]{:S(2)}, u32[]{:S(2)}) collective-permute-start(bf16[2,2,128,128]{3,2,1,0:T(8,128)(2,1)S(1)} %get-tuple-element.55), channel_id=1, source_target_pairs={{0,14},{2,4},{4,2},{6,8},{8,6},{10,12},{12,10},{14,0},{16,30},{18,... | collective-permute-start | bytes 393224 | tf_op jit(solution)/shard_map/ppermute | solution.py:315
  53.6 6.1 %collective-permute-start.14 = (bf16[2,2,128,128]{3,2,1,0:T(8,128)(2,1)S(1)}, bf16[2,2,128,128]{3,2,1,0:T(8,128)(2,1)S(1)}, u32[]{:S(2)}, u32[]{:S(2)}) collective-permute-start(bf16[2,2,128,128]{3,2,1,0:T(8,128)(2,1)S(1)} %get-tuple-element.57), channel_id=1, source_target_pairs={{0,2},{2,0},{4,6},{6,4},{8,10},{10,8},{12,14},{14,12},{16,18},{18,... | collective-permute-start | bytes 393224 | tf_op jit(solution)/shard_map/ppermute | solution.py:311
  54.4 28.1 %collective-permute-start.19 = (bf16[1024,128]{1,0:T(8,128)(2,1)S(1)}, bf16[1024,128]{1,0:T(8,128)(2,1)S(1)}, u32[]{:S(2)}, u32[]{:S(2)}) collective-permute-start(bf16[1024,128]{1,0:T(8,128)(2,1)S(1)} %get-tuple-element.65), channel_id=1, source_target_pairs={{0,48},{2,50},{4,52},{6,54},{8,56},{10,58},{12,60},{14,62},{16,32}... | collective-permute-start | bytes 786440 | tf_op jit(solution)/shard_map/ppermute | solution.py:363
  59.8 10.2 %collective-permute-start.15 = (bf16[4,2,128,128]{3,2,1,0:T(8,128)(2,1)S(1)}, bf16[4,2,128,128]{3,2,1,0:T(8,128)(2,1)S(1)}, u32[]{:S(2)}, u32[]{:S(2)}) collective-permute-start(bf16[4,2,128,128]{3,2,1,0:T(8,128)(2,1)S(1)} %pad_maximum_fusion.4.refs_1_), channel_id=1, source_target_pairs={{0,14},{2,4},{4,2},{6,8},{8,6},{10,12},{12,10},{14,0},{16,30},{18,... | collective-permute-start | bytes 786440 | tf_op jit(solution)/shard_map/ppermute | solution.py:315
  63.4 6.9 %collective-permute-start.16 = (bf16[4,2,128,128]{3,2,1,0:T(8,128)(2,1)S(1)}, bf16[4,2,128,128]{3,2,1,0:T(8,128)(2,1)S(1)}, u32[]{:S(2)}, u32[]{:S(2)}) collective-permute-start(bf16[4,2,128,128]{3,2,1,0:T(8,128)(2,1)S(1)} %pad_maximum_fusion.3.refs_0_), channel_id=1, source_target_pairs={{0,2},{2,0},{4,6},{6,4},{8,10},{10,8},{12,14},{14,12},{16,18},{18,... | collective-permute-start | bytes 786440 | tf_op jit(solution)/shard_map/ppermute | solution.py:311
  70.1 8.6 %collective-permute-start.18 = (bf16[4,2,128,128]{3,2,1,0:T(8,128)(2,1)S(1)}, bf16[4,2,128,128]{3,2,1,0:T(8,128)(2,1)S(1)}, u32[]{:S(2)}, u32[]{:S(2)}) collective-permute-start(bf16[4,2,128,128]{3,2,1,0:T(8,128)(2,1)S(1)} %add_convert_fusion.3.refs_0_), channel_id=1, source_target_pairs={{0,2},{2,0},{4,6},{6,4},{8,10},{10,8},{12,14},{14,12},{16,18},{18,... | collective-permute-start | bytes 786440 | tf_op jit(solution)/shard_map/ppermute | solution.py:311
  70.4 11.9 %collective-permute-start.17 = (bf16[4,2,128,128]{3,2,1,0:T(8,128)(2,1)S(1)}, bf16[4,2,128,128]{3,2,1,0:T(8,128)(2,1)S(1)}, u32[]{:S(2)}, u32[]{:S(2)}) collective-permute-start(bf16[4,2,128,128]{3,2,1,0:T(8,128)(2,1)S(1)} %add_convert_fusion.2.refs_1_), channel_id=1, source_target_pairs={{0,14},{2,4},{4,2},{6,8},{8,6},{10,12},{12,10},{14,0},{16,30},{18,... | collective-permute-start | bytes 786440 | tf_op jit(solution)/shard_map/ppermute | solution.py:315
  78.8 8.5 %collective-permute-start.22 = (bf16[4,2,128,128]{3,2,1,0:T(8,128)(2,1)S(1)}, bf16[4,2,128,128]{3,2,1,0:T(8,128)(2,1)S(1)}, u32[]{:S(2)}, u32[]{:S(2)}) collective-permute-start(bf16[4,2,128,128]{3,2,1,0:T(8,128)(2,1)S(1)} %add_convert_fusion.refs_1_), channel_id=1, source_target_pairs={{0,14},{2,4},{4,2},{6,8},{8,6},{10,12},{12,10},{14,0},{16,30},{18,... | collective-permute-start | bytes 786440 | tf_op jit(solution)/shard_map/ppermute | solution.py:315
  82.4 6.5 %collective-permute-start.21 = (bf16[4,2,128,128]{3,2,1,0:T(8,128)(2,1)S(1)}, bf16[4,2,128,128]{3,2,1,0:T(8,128)(2,1)S(1)}, u32[]{:S(2)}, u32[]{:S(2)}) collective-permute-start(bf16[4,2,128,128]{3,2,1,0:T(8,128)(2,1)S(1)} %add_convert_fusion.1.refs_0_), channel_id=1, source_target_pairs={{0,2},{2,0},{4,6},{6,4},{8,10},{10,8},{12,14},{14,12},{16,18},{18,... | collective-permute-start | bytes 786440 | tf_op jit(solution)/shard_map/ppermute | solution.py:311
  86.3 7.7 %collective-permute-start.20 = (bf16[1024,128]{1,0:T(8,128)(2,1)S(1)}, bf16[1024,128]{1,0:T(8,128)(2,1)S(1)}, u32[]{:S(2)}, u32[]{:S(2)}) collective-permute-start(bf16[1024,128]{1,0:T(8,128)(2,1)S(1)} %get-tuple-element.68), channel_id=1, source_target_pairs={{0,48},{2,50},{4,52},{6,54},{8,56},{10,58},{12,60},{14,62},{16,32}... | collective-permute-start | bytes 786440 | tf_op jit(solution)/shard_map/ppermute | solution.py:380
  89.0 5.8 %collective-permute-start.23 = (bf16[2,128,128]{2,1,0:T(8,128)(2,1)S(1)}, bf16[2,128,128]{2,1,0:T(8,128)(2,1)S(1)}, u32[]{:S(2)}, u32[]{:S(2)}) collective-permute-start(bf16[2,128,128]{2,1,0:T(8,128)(2,1)S(1)} %get-tuple-element.88), channel_id=1, source_target_pairs={{0,16},{2,18},{4,20},{6,22},{8,24},{10,26},{12,28},{14,30},{16,0},... | collective-permute-start | bytes 196616 | tf_op jit(solution)/shard_map/ppermute | solution.py:389
  89.7 5.5 %collective-permute-start.25 = (bf16[2,128,128]{2,1,0:T(8,128)(2,1)S(1)}, bf16[2,128,128]{2,1,0:T(8,128)(2,1)S(1)}, u32[]{:S(2)}, u32[]{:S(2)}) collective-permute-start(bf16[2,128,128]{2,1,0:T(8,128)(2,1)S(1)} %get-tuple-element.89), channel_id=1, source_target_pairs={{0,48},{2,50},{4,52},{6,54},{8,56},{10,58},{12,60},{14,62},{16,32}... | collective-permute-start | bytes 196616 | tf_op jit(solution)/shard_map/ppermute | solution.py:389
  92.5 5.8 %collective-permute-start.24 = (bf16[2,128,128]{2,1,0:T(8,128)(2,1)S(1)}, bf16[2,128,128]{2,1,0:T(8,128)(2,1)S(1)}, u32[]{:S(2)}, u32[]{:S(2)}) collective-permute-start(bf16[2,128,128]{2,1,0:T(8,128)(2,1)S(1)} %get-tuple-element.90), channel_id=1, source_target_pairs={{0,32},{2,34},{4,36},{6,38},{8,40},{10,42},{12,44},{14,46},{16,48}... | collective-permute-start | bytes 196616 | tf_op jit(solution)/shard_map/ppermute | solution.py:389
  (7 other events, 19.0 us)

commit v2 on v1

--- a/solution.py
+++ b/solution.py
@@ -128,20 +128,13 @@
     def each_unit(facts, work):
         def step(unit, _):
             one, two = is_live(unit, facts)
-            clear = is_clear(unit, facts) & one & two
-            whole = pl.ds(0, 2 * block)
-            pl.when(clear)(lambda: work(unit, whole, False))
+            both, whole = one & two, pl.ds(0, 2 * block)
             if kind == "own":
-
-                def half_step(half, _):
-                    live = jnp.where(half == 0, one, two) & jnp.logical_not(clear)
-                    rows = pl.ds(pl.multiple_of(half * block, block), block)
-                    pl.when(live)(lambda: work(unit, rows, True))
-                    return 0
-
-                lax.fori_loop(0, 2, half_step, 0)
-                return 0
-            pl.when(one & two & jnp.logical_not(clear))(lambda: work(unit, whole, True))
+                pl.when(both)(lambda: work(unit, whole, True))
+            else:
+                clear = is_clear(unit, facts)
+                pl.when(both & clear)(lambda: work(unit, whole, False))
+                pl.when(both & jnp.logical_not(clear))(lambda: work(unit, whole, True))
             half = pl.ds(pl.multiple_of(jnp.where(one, 0, block), block), block)
             pl.when(one ^ two)(lambda: work(unit, half, True))
             return 0

time: 100 us -> 98.8 us (0.988)
  Pallas kernels: 31.8 us -> 33.5 us
  starting transfers between devices: 39 us -> 37.7 us
  waiting for transfers between devices: 21.4 us -> 20.4 us
    pallas_call x9, Pallas kernels: 31.8 us -> 33.5 us  [run_stage(): pl.pallas_call(functools.partial(stage_kernel, stage, len(after), len(pas...]
    ppermute x8, starting transfers between devices: 4.56 us -> 2.88 us  [swap_even(): return lax.ppermute(array, 'ctx', swap_z(0))]
  transfers between devices with their start and end apart: 26 -> 26, of which waited for: 15 -> 15; matrix products, arithmetic and copies ran while one was open for 3% -> 3% of each run, Pallas kernels for 27% -> 29%
where the time goes in v2:
time: 98.8 us; the launch traced here: 99.3 us
  starting transfers between devices  37.7 us (38%)
  Pallas kernels  33.5 us (34%)
  waiting for transfers between devices  20.4 us (21%)
  local copies, waits for them, and re-layouts  3.84 us (4%)
  other arithmetic  2.75 us (3%)
  between operations  1.02 us (1%)
    pallas_call x9, Pallas kernels, run_stage(): pl.pallas_call(functools.partial(stage_kernel, stage, len(after), len(pas...  33.5 us
    ppermute x8, starting transfers between devices, swap_odd(): return lax.ppermute(array, 'ctx', swap_z(1))  19.6 us
    ppermute x8, waiting for transfers between devices, swap_even(): return lax.ppermute(array, 'ctx', swap_z(0))  7.42 us
    ppermute x8, waiting for transfers between devices, swap_odd(): return lax.ppermute(array, 'ctx', swap_z(1))  6.94 us
    ppermute x3, starting transfers between devices, on_device(): lax.ppermute(pairs[mask // 2], 'ctx', swap_y(mask))  4.43 us
    ppermute x3, starting transfers between devices, on_device(): lax.ppermute(sums[slot].astype(jnp.bfloat16), 'ctx', swap_y(mask))  4.18 us
    unnamed x12, local copies, waits for them, and re-layouts  3.59 us
    ppermute x3, waiting for transfers between devices, on_device(): lax.ppermute(sums[slot].astype(jnp.bfloat16), 'ctx', swap_y(mask))  2.93 us
  transfers between devices with their start and end apart: 26, of which 15 were waited for; matrix products, arithmetic and copies ran while one was open for 3% of the time, Pallas kernels for 29%

profile of v2, /device:TPU:6, one launch (start us, length us, event | category | flops | bytes accessed | tf_op | source)
XLA Modules:
  0.0 99.3 jit_solution(5051514658193443719)
XLA Ops:
  2.5 3.3 %collective-permute-start.3 = (bf16[2,128,128]{2,1,0:T(8,128)(2,1)S(1)}, bf16[2,128,128]{2,1,0:T(8,128)(2,1)S(1)}, u32[]{:S(2)}, u32[]{:S(2)}) collective-permute-start(bf16[2,128,128]{2,1,0:T(8,128)(2,1)S(1)} %pad_maximum_fusion.7), channel_id=1, source_target_pairs={{0,32},{2,34},{4,36},{6,38},{8,40},{10,42},{12,44},{14,46},{16,48}... | collective-permute-start | bytes 196616 | tf_op jit(solution)/shard_map/ppermute | solution.py:327
  7.0 2.3 %collective-permute-start = (bf16[1024,128]{1,0:T(8,128)(2,1)S(1)}, bf16[1024,128]{1,0:T(8,128)(2,1)S(1)}, u32[]{:S(2)}, u32[]{:S(2)}) collective-permute-start(bf16[1024,128]{1,0:T(8,128)(2,1)S(1)} %get-tuple-element.86), channel_id=1, source_target_pairs={{0,48},{2,50},{4,52},{6,54},{8,56},{10,58},{12,60},{14,62},{16,32}... | collective-permute-start | bytes 786440 | tf_op jit(solution)/shard_map/ppermute | solution.py:330
  11.9 2.0 %collective-permute-start.9 = (bf16[4,2,128,128]{3,2,1,0:T(8,128)(2,1)S(1)}, bf16[4,2,128,128]{3,2,1,0:T(8,128)(2,1)S(1)}, u32[]{:S(2)}, u32[]{:S(2)}) collective-permute-start(bf16[4,2,128,128]{3,2,1,0:T(8,128)(2,1)S(1)} %pad_maximum_fusion.2.refs_4_.refs_8_), channel_id=1, source_target_pairs={{0,2},{2,0},{4,6},{6,4},{8,10},{10,8},{12,14},{14,12},{16,18},{18,... | collective-permute-start | bytes 786440 | tf_op jit(solution)/shard_map/ppermute | solution.py:304
  13.9 4.9 %collective-permute-start.5 = (bf16[4,2,128,128]{3,2,1,0:T(8,128)(2,1)S(1)}, bf16[4,2,128,128]{3,2,1,0:T(8,128)(2,1)S(1)}, u32[]{:S(2)}, u32[]{:S(2)}) collective-permute-start(bf16[4,2,128,128]{3,2,1,0:T(8,128)(2,1)S(1)} %pad_maximum_fusion.2.refs_4_.refs_8_), channel_id=1, source_target_pairs={{0,14},{2,4},{4,2},{6,8},{8,6},{10,12},{12,10},{14,0},{16,30},{18,... | collective-permute-start | bytes 786440 | tf_op jit(solution)/shard_map/ppermute | solution.py:308
  19.6 2.8 %fwdown.1 = (f32[2,8,1024]{2,1,0:T(8,128)S(1)}, f32[2,8,1024]{2,1,0:T(8,128)S(1)}, f32[2,128,1024]{2,1,0:T(8,128)S(1)}, bf16[1024,128]{1,0:T(8,128)(2,1)S(1)}) custom-call(s32[16]{0:T(128)S(1)} %copy-done, s32[3]{0:T(128)S(1)} %get-tuple-element.105.refs_1_.refs_3_, ...), custom_call_target="tpu_custom_call", output_to_operand_aliasing={{3}: (5, {})} | custom-call | flops 1610612736 | bytes 4194304 | tf_op jit(solution)/shard_map/fwdown/pallas_call | solution.py:270
  24.0 2.4 %collective-permute-start.10 = (bf16[4,2,128,128]{3,2,1,0:T(8,128)(2,1)S(1)}, bf16[4,2,128,128]{3,2,1,0:T(8,128)(2,1)S(1)}, u32[]{:S(2)}, u32[]{:S(2)}) collective-permute-start(bf16[4,2,128,128]{3,2,1,0:T(8,128)(2,1)S(1)} %collective-permute-done.9.refs_4_.refs_8_), channel_id=1, source_target_pairs={{0,14},{2,4},{4,2},{6,8},{8,6},{10,12},{12,10},{14,0},{16,30},{18,... | collective-permute-start | bytes 786440 | tf_op jit(solution)/shard_map/ppermute | solution.py:308
  26.4 3.3 %fwdpair.3 = (f32[2,8,1024]{2,1,0:T(8,128)S(1)}, f32[2,8,1024]{2,1,0:T(8,128)S(1)}, f32[2,128,1024]{2,1,0:T(8,128)S(1)}) custom-call(s32[16]{0:T(128)S(1)} %copy-done, s32[3]{0:T(128)S(1)} %get-tuple-element.76.refs_1_.refs_3_, bf16[1024,128]{1,0:T(8,128)(2,1)S(1)} %get-tuple-element.87.refs_2_.refs_4_, ...), custom_call_target="tpu_custom_call", output_to_operand_aliasing={{0}: (6, {}), {1}: (7, {}), {2}: (8, {})} | custom-call | flops 3221225472 | bytes 4194304 | tf_op jit(solution)/shard_map/fwdpair/pallas_call | solution.py:270
  29.7 1.9 %collective-permute-done.10.refs_5_.refs_9_ = bf16[4,2,128,128]{3,2,1,0:T(8,128)(2,1)S(1)} collective-permute-done((bf16[4,2,128,128]{3,2,1,0:T(8,128)(2,1)S(1)}, bf16[4,2,128,128]{3,2,1,0:T(8,128)(2,1)S(1)}, u32[]{:S(2)}, u32[]{:S(2)}) %collective-permute-start.10) | collective-permute-done | bytes 262176 | tf_op jit(solution)/shard_map/ppermute | solution.py:308
  31.6 3.1 %collective-permute-done.6.refs_4_.refs_8_ = bf16[4,2,128,128]{3,2,1,0:T(8,128)(2,1)S(1)} collective-permute-done((bf16[4,2,128,128]{3,2,1,0:T(8,128)(2,1)S(1)}, bf16[4,2,128,128]{3,2,1,0:T(8,128)(2,1)S(1)}, u32[]{:S(2)}, u32[]{:S(2)}) %collective-permute-start.6) | collective-permute-done | bytes 262176 | tf_op jit(solution)/shard_map/ppermute | solution.py:304
  34.6 3.3 %fwdpair.4 = (f32[2,8,1024]{2,1,0:T(8,128)S(1)}, f32[2,8,1024]{2,1,0:T(8,128)S(1)}, f32[2,128,1024]{2,1,0:T(8,128)S(1)}) custom-call(s32[16]{0:T(128)S(1)} %copy-done, s32[3]{0:T(128)S(1)} %get-tuple-element.103.refs_1_.refs_3_, bf16[1024,128]{1,0:T(8,128)(2,1)S(1)} %get-tuple-element.87.refs_2_.refs_4_, ...), custom_call_target="tpu_custom_call", output_to_operand_aliasing={{0}: (6, {}), {1}: (7, {}), {2}: (8, {})} | custom-call | flops 3221225472 | bytes 4194304 | tf_op jit(solution)/shard_map/fwdpair/pallas_call | solution.py:270
  38.4 2.0 %collective-permute-start.12 = (bf16[2,2,128,128]{3,2,1,0:T(8,128)(2,1)S(1)}, bf16[2,2,128,128]{3,2,1,0:T(8,128)(2,1)S(1)}, u32[]{:S(2)}, u32[]{:S(2)}) collective-permute-start(bf16[2,2,128,128]{3,2,1,0:T(8,128)(2,1)S(1)} %slice.92), channel_id=1, source_target_pairs={{0,14},{2,4},{4,2},{6,8},{8,6},{10,12},{12,10},{14,0},{16,30},{18,... | collective-permute-start | bytes 393224 | tf_op jit(solution)/shard_map/ppermute | solution.py:308
  40.5 3.2 %collective-permute-done.7.refs_5_.refs_7_ = bf16[4,2,128,128]{3,2,1,0:T(8,128)(2,1)S(1)} collective-permute-done((bf16[4,2,128,128]{3,2,1,0:T(8,128)(2,1)S(1)}, bf16[4,2,128,128]{3,2,1,0:T(8,128)(2,1)S(1)}, u32[]{:S(2)}, u32[]{:S(2)}) %collective-permute-start.7) | collective-permute-done | bytes 262176 | tf_op jit(solution)/shard_map/ppermute | solution.py:308
  43.9 3.3 %fwdpair.5 = (f32[2,8,1024]{2,1,0:T(8,128)S(1)}, f32[2,8,1024]{2,1,0:T(8,128)S(1)}, f32[2,128,1024]{2,1,0:T(8,128)S(1)}) custom-call(s32[16]{0:T(128)S(1)} %copy-done, s32[3]{0:T(128)S(1)} %get-tuple-element.104.refs_1_, bf16[1024,128]{1,0:T(8,128)(2,1)S(1)} %get-tuple-element.87.refs_2_.refs_4_, ...), custom_call_target="tpu_custom_call", output_to_operand_aliasing={{0}: (6, {}), {1}: (7, {}), {2}: (8, {})} | custom-call | flops 3221225472 | bytes 4194304 | tf_op jit(solution)/shard_map/fwdpair/pallas_call | solution.py:270
  48.9 4.8 %fwdbwdfar.1 = (bf16[1024,128]{1,0:T(8,128)(2,1)S(1)}, bf16[1024,128]{1,0:T(8,128)(2,1)S(1)}, f32[2,8,1024]{2,1,0:T(8,128)S(1)}, f32[2,8,1024]{2,1,0:T(8,128)S(1...) custom-call(s32[16]{0:T(128)S(1)} %copy-done, ...), custom_call_target="tpu_custom_call" | custom-call | flops 5637144576 | bytes 4194304 | tf_op jit(solution)/shard_map/fwdbwdfar/pallas_call | solution.py:270
  55.7 4.1 %bwdpair.3 = (f32[2,128,1024]{2,1,0:T(8,128)S(1)}, bf16[4,2,128,128]{3,2,1,0:T(8,128)(2,1)S(1)}, bf16[4,2,128,128]{3,2,1,0:T(8,128)(2,1)S(1)}) custom-call(s32[16]{0:T(128)S(1)} %copy-done, s32[3]{0:T(128)S(1)} %get-tuple-element.104.refs_1_, bf16[1024,128]{1,0:T(8,128)(2,1)S(1)} %get-tuple-element.87.refs_2_.refs_4_, ...), custom_call_target="tpu_custom_call", output_to_operand_aliasing={{0}: (10, {})} | custom-call | flops 8053063680 | bytes 4194304 | tf_op jit(solution)/shard_map/bwdpair/pallas_call | solution.py:270
  60.1 3.5 %collective-permute-start.15 = (bf16[4,2,128,128]{3,2,1,0:T(8,128)(2,1)S(1)}, bf16[4,2,128,128]{3,2,1,0:T(8,128)(2,1)S(1)}, u32[]{:S(2)}, u32[]{:S(2)}) collective-permute-start(bf16[4,2,128,128]{3,2,1,0:T(8,128)(2,1)S(1)} %pad_maximum_fusion.4.refs_1_), channel_id=1, source_target_pairs={{0,14},{2,4},{4,2},{6,8},{8,6},{10,12},{12,10},{14,0},{16,30},{18,... | collective-permute-start | bytes 786440 | tf_op jit(solution)/shard_map/ppermute | solution.py:308
  64.0 4.1 %bwdpair.4 = (f32[2,128,1024]{2,1,0:T(8,128)S(1)}, bf16[4,2,128,128]{3,2,1,0:T(8,128)(2,1)S(1)}, bf16[4,2,128,128]{3,2,1,0:T(8,128)(2,1)S(1)}) custom-call(bf16[4,2,128,128]{3,2,1,0:T(8,128)(2,1)S(1)} %pad_maximum_fusion.3.refs_0_, bf16[4,2,128,128]{3,2,1,0:T(8,128)(2,1)S(1)} %pad_maximum_fusion.4.refs_1_, ...), custom_call_target="tpu_custom_call", output_to_operand_aliasing={{0}: (12, {})} | custom-call | flops 8053063680 | bytes 4194304 | tf_op jit(solution)/shard_map/bwdpair/pallas_call | solution.py:270
  68.1 1.9 %collective-permute-done.15 = bf16[4,2,128,128]{3,2,1,0:T(8,128)(2,1)S(1)} collective-permute-done((bf16[4,2,128,128]{3,2,1,0:T(8,128)(2,1)S(1)}, bf16[4,2,128,128]{3,2,1,0:T(8,128)(2,1)S(1)}, u32[]{:S(2)}, u32[]{:S(2)}) %collective-permute-start.15) | collective-permute-done | bytes 262176 | tf_op jit(solution)/shard_map/ppermute | solution.py:308
  70.7 3.3 %collective-permute-start.17 = (bf16[4,2,128,128]{3,2,1,0:T(8,128)(2,1)S(1)}, bf16[4,2,128,128]{3,2,1,0:T(8,128)(2,1)S(1)}, u32[]{:S(2)}, u32[]{:S(2)}) collective-permute-start(bf16[4,2,128,128]{3,2,1,0:T(8,128)(2,1)S(1)} %add_convert_fusion.2.refs_1_), channel_id=1, source_target_pairs={{0,14},{2,4},{4,2},{6,8},{8,6},{10,12},{12,10},{14,0},{16,30},{18,... | collective-permute-start | bytes 786440 | tf_op jit(solution)/shard_map/ppermute | solution.py:308
  74.0 4.1 %bwdpair.5 = (f32[2,128,1024]{2,1,0:T(8,128)S(1)}, bf16[4,2,128,128]{3,2,1,0:T(8,128)(2,1)S(1)}, bf16[4,2,128,128]{3,2,1,0:T(8,128)(2,1)S(1)}) custom-call(bf16[4,2,128,128]{3,2,1,0:T(8,128)(2,1)S(1)} %add_convert_fusion.3.refs_0_, bf16[4,2,128,128]{3,2,1,0:T(8,128)(2,1)S(1)} %add_convert_fusion.2.refs_1_, ...), custom_call_target="tpu_custom_call", output_to_operand_aliasing={{0}: (12, {})} | custom-call | flops 8053063680 | bytes 4194304 | tf_op jit(solution)/shard_map/bwdpair/pallas_call | solution.py:270
  79.0 3.3 %collective-permute-start.22 = (bf16[4,2,128,128]{3,2,1,0:T(8,128)(2,1)S(1)}, bf16[4,2,128,128]{3,2,1,0:T(8,128)(2,1)S(1)}, u32[]{:S(2)}, u32[]{:S(2)}) collective-permute-start(bf16[4,2,128,128]{3,2,1,0:T(8,128)(2,1)S(1)} %add_convert_fusion.refs_1_), channel_id=1, source_target_pairs={{0,14},{2,4},{4,2},{6,8},{8,6},{10,12},{12,10},{14,0},{16,30},{18,... | collective-permute-start | bytes 786440 | tf_op jit(solution)/shard_map/ppermute | solution.py:308
  82.5 3.7 %bwdown.1 = (bf16[1024,128]{1,0:T(8,128)(2,1)S(1)}, bf16[1024,128]{1,0:T(8,128)(2,1)S(1)}, bf16[4,2,128,128]{3,2,1,0:T(8,128)(2,1)S(1)}, bf16[1024,128]{1,0:T(8,128)(2,1)S(1)}) custom-call(bf16[4,2,128,128]{3,2,1,0:T(8,128)(2,1)S(1)} %add_convert_fusion.1.refs_0_, ...), custom_call_target="tpu_custom_call", output_to_operand_aliasing={{3}: (12, {})} | custom-call | flops 4026531840 | bytes 4194304 | tf_op jit(solution)/shard_map/bwdown/pallas_call | solution.py:270
  89.8 2.2 %collective-permute-start.25 = (bf16[2,128,128]{2,1,0:T(8,128)(2,1)S(1)}, bf16[2,128,128]{2,1,0:T(8,128)(2,1)S(1)}, u32[]{:S(2)}, u32[]{:S(2)}) collective-permute-start(bf16[2,128,128]{2,1,0:T(8,128)(2,1)S(1)} %get-tuple-element.89), channel_id=1, source_target_pairs={{0,48},{2,50},{4,52},{6,54},{8,56},{10,58},{12,60},{14,62},{16,32}... | collective-permute-start | bytes 196616 | tf_op jit(solution)/shard_map/ppermute | solution.py:382
  95.3 2.5 %collective-permute-done.24 = bf16[2,128,128]{2,1,0:T(8,128)(2,1)S(1)} collective-permute-done((bf16[2,128,128]{2,1,0:T(8,128)(2,1)S(1)}, bf16[2,128,128]{2,1,0:T(8,128)(2,1)S(1)}, u32[]{:S(2)}, u32[]{:S(2)}) %collective-permute-start.24) | collective-permute-done | bytes 65568 | tf_op jit(solution)/shard_map/ppermute | solution.py:382
  (79 shorter events, 23.0 us)
Async XLA Ops:
  2.5 8.7 %collective-permute-start.3 = (bf16[2,128,128]{2,1,0:T(8,128)(2,1)S(1)}, bf16[2,128,128]{2,1,0:T(8,128)(2,1)S(1)}, u32[]{:S(2)}, u32[]{:S(2)}) collective-permute-start(bf16[2,128,128]{2,1,0:T(8,128)(2,1)S(1)} %pad_maximum_fusion.7), channel_id=1, source_target_pairs={{0,32},{2,34},{4,36},{6,38},{8,40},{10,42},{12,44},{14,46},{16,48}... | collective-permute-start | bytes 196616 | tf_op jit(solution)/shard_map/ppermute | solution.py:327
  5.7 6.1 %collective-permute-start.2 = (bf16[2,128,128]{2,1,0:T(8,128)(2,1)S(1)}, bf16[2,128,128]{2,1,0:T(8,128)(2,1)S(1)}, u32[]{:S(2)}, u32[]{:S(2)}) collective-permute-start(bf16[2,128,128]{2,1,0:T(8,128)(2,1)S(1)} %pad_maximum_fusion.7), channel_id=1, source_target_pairs={{0,48},{2,50},{4,52},{6,54},{8,56},{10,58},{12,60},{14,62},{16,32}... | collective-permute-start | bytes 196616 | tf_op jit(solution)/shard_map/ppermute | solution.py:327
  7.0 11.9 %collective-permute-start = (bf16[1024,128]{1,0:T(8,128)(2,1)S(1)}, bf16[1024,128]{1,0:T(8,128)(2,1)S(1)}, u32[]{:S(2)}, u32[]{:S(2)}) collective-permute-start(bf16[1024,128]{1,0:T(8,128)(2,1)S(1)} %get-tuple-element.86), channel_id=1, source_target_pairs={{0,48},{2,50},{4,52},{6,54},{8,56},{10,58},{12,60},{14,62},{16,32}... | collective-permute-start | bytes 786440 | tf_op jit(solution)/shard_map/ppermute | solution.py:330
  11.9 12.1 %collective-permute-start.9 = (bf16[4,2,128,128]{3,2,1,0:T(8,128)(2,1)S(1)}, bf16[4,2,128,128]{3,2,1,0:T(8,128)(2,1)S(1)}, u32[]{:S(2)}, u32[]{:S(2)}) collective-permute-start(bf16[4,2,128,128]{3,2,1,0:T(8,128)(2,1)S(1)} %pad_maximum_fusion.2.refs_4_.refs_8_), channel_id=1, source_target_pairs={{0,2},{2,0},{4,6},{6,4},{8,10},{10,8},{12,14},{14,12},{16,18},{18,... | collective-permute-start | bytes 786440 | tf_op jit(solution)/shard_map/ppermute | solution.py:304
  13.9 12.5 %collective-permute-start.5 = (bf16[4,2,128,128]{3,2,1,0:T(8,128)(2,1)S(1)}, bf16[4,2,128,128]{3,2,1,0:T(8,128)(2,1)S(1)}, u32[]{:S(2)}, u32[]{:S(2)}) collective-permute-start(bf16[4,2,128,128]{3,2,1,0:T(8,128)(2,1)S(1)} %pad_maximum_fusion.2.refs_4_.refs_8_), channel_id=1, source_target_pairs={{0,14},{2,4},{4,2},{6,8},{8,6},{10,12},{12,10},{14,0},{16,30},{18,... | collective-permute-start | bytes 786440 | tf_op jit(solution)/shard_map/ppermute | solution.py:308
  22.4 24.9 %collective-permute-start.4 = (bf16[1024,128]{1,0:T(8,128)(2,1)S(1)}, bf16[1024,128]{1,0:T(8,128)(2,1)S(1)}, u32[]{:S(2)}, u32[]{:S(2)}) collective-permute-start(bf16[1024,128]{1,0:T(8,128)(2,1)S(1)} %get-tuple-element.37), channel_id=1, source_target_pairs={{0,48},{2,50},{4,52},{6,54},{8,56},{10,58},{12,60},{14,62},{16,32}... | collective-permute-start | bytes 786440 | tf_op jit(solution)/shard_map/ppermute | solution.py:349
  24.0 7.6 %collective-permute-start.10 = (bf16[4,2,128,128]{3,2,1,0:T(8,128)(2,1)S(1)}, bf16[4,2,128,128]{3,2,1,0:T(8,128)(2,1)S(1)}, u32[]{:S(2)}, u32[]{:S(2)}) collective-permute-start(bf16[4,2,128,128]{3,2,1,0:T(8,128)(2,1)S(1)} %collective-permute-done.9.refs_4_.refs_8_), channel_id=1, source_target_pairs={{0,14},{2,4},{4,2},{6,8},{8,6},{10,12},{12,10},{14,0},{16,30},{18,... | collective-permute-start | bytes 786440 | tf_op jit(solution)/shard_map/ppermute | solution.py:308
  26.4 8.2 %collective-permute-start.6 = (bf16[4,2,128,128]{3,2,1,0:T(8,128)(2,1)S(1)}, bf16[4,2,128,128]{3,2,1,0:T(8,128)(2,1)S(1)}, u32[]{:S(2)}, u32[]{:S(2)}) collective-permute-start(bf16[4,2,128,128]{3,2,1,0:T(8,128)(2,1)S(1)} %collective-permute-done.5.refs_5_.refs_9_), channel_id=1, source_target_pairs={{0,2},{2,0},{4,6},{6,4},{8,10},{10,8},{12,14},{14,12},{16,18},{18,... | collective-permute-start | bytes 786440 | tf_op jit(solution)/shard_map/ppermute | solution.py:304
  31.6 6.8 %collective-permute-start.11 = (bf16[4,2,128,128]{3,2,1,0:T(8,128)(2,1)S(1)}, bf16[4,2,128,128]{3,2,1,0:T(8,128)(2,1)S(1)}, u32[]{:S(2)}, u32[]{:S(2)}) collective-permute-start(bf16[4,2,128,128]{3,2,1,0:T(8,128)(2,1)S(1)} %collective-permute-done.10.refs_5_.refs_9_), channel_id=1, source_target_pairs={{0,2},{2,0},{4,6},{6,4},{8,10},{10,8},{12,14},{14,12},{16,18},{18,... | collective-permute-start | bytes 786440 | tf_op jit(solution)/shard_map/ppermute | solution.py:304
  34.6 9.0 %collective-permute-start.7 = (bf16[4,2,128,128]{3,2,1,0:T(8,128)(2,1)S(1)}, bf16[4,2,128,128]{3,2,1,0:T(8,128)(2,1)S(1)}, u32[]{:S(2)}, u32[]{:S(2)}) collective-permute-start(bf16[4,2,128,128]{3,2,1,0:T(8,128)(2,1)S(1)} %collective-permute-done.6.refs_4_.refs_8_), channel_id=1, source_target_pairs={{0,14},{2,4},{4,2},{6,8},{8,6},{10,12},{12,10},{14,0},{16,30},{18,... | collective-permute-start | bytes 786440 | tf_op jit(solution)/shard_map/ppermute | solution.py:308
  38.4 8.9 %collective-permute-start.12 = (bf16[2,2,128,128]{3,2,1,0:T(8,128)(2,1)S(1)}, bf16[2,2,128,128]{3,2,1,0:T(8,128)(2,1)S(1)}, u32[]{:S(2)}, u32[]{:S(2)}) collective-permute-start(bf16[2,2,128,128]{3,2,1,0:T(8,128)(2,1)S(1)} %slice.92), channel_id=1, source_target_pairs={{0,14},{2,4},{4,2},{6,8},{8,6},{10,12},{12,10},{14,0},{16,30},{18,... | collective-permute-start | bytes 393224 | tf_op jit(solution)/shard_map/ppermute | solution.py:308
  53.7 9.9 %collective-permute-start.13 = (bf16[2,2,128,128]{3,2,1,0:T(8,128)(2,1)S(1)}, bf16[2,2,128,128]{3,2,1,0:T(8,128)(2,1)S(1)}, u32[]{:S(2)}, u32[]{:S(2)}) collective-permute-start(bf16[2,2,128,128]{3,2,1,0:T(8,128)(2,1)S(1)} %get-tuple-element.55), channel_id=1, source_target_pairs={{0,14},{2,4},{4,2},{6,8},{8,6},{10,12},{12,10},{14,0},{16,30},{18,... | collective-permute-start | bytes 393224 | tf_op jit(solution)/shard_map/ppermute | solution.py:308
  53.8 6.2 %collective-permute-start.14 = (bf16[2,2,128,128]{3,2,1,0:T(8,128)(2,1)S(1)}, bf16[2,2,128,128]{3,2,1,0:T(8,128)(2,1)S(1)}, u32[]{:S(2)}, u32[]{:S(2)}) collective-permute-start(bf16[2,2,128,128]{3,2,1,0:T(8,128)(2,1)S(1)} %get-tuple-element.57), channel_id=1, source_target_pairs={{0,2},{2,0},{4,6},{6,4},{8,10},{10,8},{12,14},{14,12},{16,18},{18,... | collective-permute-start | bytes 393224 | tf_op jit(solution)/shard_map/ppermute | solution.py:304
  53.9 28.6 %collective-permute-start.19 = (bf16[1024,128]{1,0:T(8,128)(2,1)S(1)}, bf16[1024,128]{1,0:T(8,128)(2,1)S(1)}, u32[]{:S(2)}, u32[]{:S(2)}) collective-permute-start(bf16[1024,128]{1,0:T(8,128)(2,1)S(1)} %get-tuple-element.65), channel_id=1, source_target_pairs={{0,48},{2,50},{4,52},{6,54},{8,56},{10,58},{12,60},{14,62},{16,32}... | collective-permute-start | bytes 786440 | tf_op jit(solution)/shard_map/ppermute | solution.py:356
  60.1 9.9 %collective-permute-start.15 = (bf16[4,2,128,128]{3,2,1,0:T(8,128)(2,1)S(1)}, bf16[4,2,128,128]{3,2,1,0:T(8,128)(2,1)S(1)}, u32[]{:S(2)}, u32[]{:S(2)}) collective-permute-start(bf16[4,2,128,128]{3,2,1,0:T(8,128)(2,1)S(1)} %pad_maximum_fusion.4.refs_1_), channel_id=1, source_target_pairs={{0,14},{2,4},{4,2},{6,8},{8,6},{10,12},{12,10},{14,0},{16,30},{18,... | collective-permute-start | bytes 786440 | tf_op jit(solution)/shard_map/ppermute | solution.py:308
  63.7 7.0 %collective-permute-start.16 = (bf16[4,2,128,128]{3,2,1,0:T(8,128)(2,1)S(1)}, bf16[4,2,128,128]{3,2,1,0:T(8,128)(2,1)S(1)}, u32[]{:S(2)}, u32[]{:S(2)}) collective-permute-start(bf16[4,2,128,128]{3,2,1,0:T(8,128)(2,1)S(1)} %pad_maximum_fusion.3.refs_0_), channel_id=1, source_target_pairs={{0,2},{2,0},{4,6},{6,4},{8,10},{10,8},{12,14},{14,12},{16,18},{18,... | collective-permute-start | bytes 786440 | tf_op jit(solution)/shard_map/ppermute | solution.py:304
  70.0 8.9 %collective-permute-start.18 = (bf16[4,2,128,128]{3,2,1,0:T(8,128)(2,1)S(1)}, bf16[4,2,128,128]{3,2,1,0:T(8,128)(2,1)S(1)}, u32[]{:S(2)}, u32[]{:S(2)}) collective-permute-start(bf16[4,2,128,128]{3,2,1,0:T(8,128)(2,1)S(1)} %add_convert_fusion.3.refs_0_), channel_id=1, source_target_pairs={{0,2},{2,0},{4,6},{6,4},{8,10},{10,8},{12,14},{14,12},{16,18},{18,... | collective-permute-start | bytes 786440 | tf_op jit(solution)/shard_map/ppermute | solution.py:304
  70.7 11.6 %collective-permute-start.17 = (bf16[4,2,128,128]{3,2,1,0:T(8,128)(2,1)S(1)}, bf16[4,2,128,128]{3,2,1,0:T(8,128)(2,1)S(1)}, u32[]{:S(2)}, u32[]{:S(2)}) collective-permute-start(bf16[4,2,128,128]{3,2,1,0:T(8,128)(2,1)S(1)} %add_convert_fusion.2.refs_1_), channel_id=1, source_target_pairs={{0,14},{2,4},{4,2},{6,8},{8,6},{10,12},{12,10},{14,0},{16,30},{18,... | collective-permute-start | bytes 786440 | tf_op jit(solution)/shard_map/ppermute | solution.py:308
  79.0 9.1 %collective-permute-start.22 = (bf16[4,2,128,128]{3,2,1,0:T(8,128)(2,1)S(1)}, bf16[4,2,128,128]{3,2,1,0:T(8,128)(2,1)S(1)}, u32[]{:S(2)}, u32[]{:S(2)}) collective-permute-start(bf16[4,2,128,128]{3,2,1,0:T(8,128)(2,1)S(1)} %add_convert_fusion.refs_1_), channel_id=1, source_target_pairs={{0,14},{2,4},{4,2},{6,8},{8,6},{10,12},{12,10},{14,0},{16,30},{18,... | collective-permute-start | bytes 786440 | tf_op jit(solution)/shard_map/ppermute | solution.py:308
  82.4 6.5 %collective-permute-start.21 = (bf16[4,2,128,128]{3,2,1,0:T(8,128)(2,1)S(1)}, bf16[4,2,128,128]{3,2,1,0:T(8,128)(2,1)S(1)}, u32[]{:S(2)}, u32[]{:S(2)}) collective-permute-start(bf16[4,2,128,128]{3,2,1,0:T(8,128)(2,1)S(1)} %add_convert_fusion.1.refs_0_), channel_id=1, source_target_pairs={{0,2},{2,0},{4,6},{6,4},{8,10},{10,8},{12,14},{14,12},{16,18},{18,... | collective-permute-start | bytes 786440 | tf_op jit(solution)/shard_map/ppermute | solution.py:304
  86.3 7.7 %collective-permute-start.20 = (bf16[1024,128]{1,0:T(8,128)(2,1)S(1)}, bf16[1024,128]{1,0:T(8,128)(2,1)S(1)}, u32[]{:S(2)}, u32[]{:S(2)}) collective-permute-start(bf16[1024,128]{1,0:T(8,128)(2,1)S(1)} %get-tuple-element.68), channel_id=1, source_target_pairs={{0,48},{2,50},{4,52},{6,54},{8,56},{10,58},{12,60},{14,62},{16,32}... | collective-permute-start | bytes 786440 | tf_op jit(solution)/shard_map/ppermute | solution.py:373
  89.0 5.8 %collective-permute-start.23 = (bf16[2,128,128]{2,1,0:T(8,128)(2,1)S(1)}, bf16[2,128,128]{2,1,0:T(8,128)(2,1)S(1)}, u32[]{:S(2)}, u32[]{:S(2)}) collective-permute-start(bf16[2,128,128]{2,1,0:T(8,128)(2,1)S(1)} %get-tuple-element.88), channel_id=1, source_target_pairs={{0,16},{2,18},{4,20},{6,22},{8,24},{10,26},{12,28},{14,30},{16,0},... | collective-permute-start | bytes 196616 | tf_op jit(solution)/shard_map/ppermute | solution.py:382
  89.8 5.5 %collective-permute-start.25 = (bf16[2,128,128]{2,1,0:T(8,128)(2,1)S(1)}, bf16[2,128,128]{2,1,0:T(8,128)(2,1)S(1)}, u32[]{:S(2)}, u32[]{:S(2)}) collective-permute-start(bf16[2,128,128]{2,1,0:T(8,128)(2,1)S(1)} %get-tuple-element.89), channel_id=1, source_target_pairs={{0,48},{2,50},{4,52},{6,54},{8,56},{10,58},{12,60},{14,62},{16,32}... | collective-permute-start | bytes 196616 | tf_op jit(solution)/shard_map/ppermute | solution.py:382
  92.0 5.8 %collective-permute-start.24 = (bf16[2,128,128]{2,1,0:T(8,128)(2,1)S(1)}, bf16[2,128,128]{2,1,0:T(8,128)(2,1)S(1)}, u32[]{:S(2)}, u32[]{:S(2)}) collective-permute-start(bf16[2,128,128]{2,1,0:T(8,128)(2,1)S(1)} %get-tuple-element.90), channel_id=1, source_target_pairs={{0,32},{2,34},{4,36},{6,38},{8,40},{10,42},{12,44},{14,46},{16,48}... | collective-permute-start | bytes 196616 | tf_op jit(solution)/shard_map/ppermute | solution.py:382
  (7 other events, 19.0 us)

commit v3 on v2

--- a/solution.py
+++ b/solution.py
@@ -382,8 +382,8 @@
         mask: lax.ppermute(sums[slot].astype(jnp.bfloat16), "ctx", swap_y(mask)).astype(jnp.float32)
         for slot, mask in ((3, 2), (2, 3), (1, 1))
     }
-    near, far = sums[0] + arrived[1], arrived[2] + arrived[3]
-    heads = [jnp.where(mine == 0, near, far), jnp.where(mine == 0, far, near)]
+    far, near = arrived[2] + arrived[3], arrived[1] + sums[0]
+    heads = [jnp.where(mine == 1, far, near), jnp.where(mine == 1, near, far)]
     grads = jnp.stack(heads, axis=2).astype(jnp.bfloat16)
     return attended, query_grad, grads[0], grads[1]
 

time: 98.8 us -> 98.9 us (level)
  Pallas kernels: 33.5 us -> 13.3 us
  waiting for transfers between devices: 20.4 us -> 40.5 us
    pallas_call x9, Pallas kernels: 33.5 us -> 13.3 us  [run_stage(): pl.pallas_call(functools.partial(stage_kernel, stage, len(after), len(pas...]
    ppermute x8, waiting for transfers between devices: 7.42 us -> 19.7 us  [swap_even(): return lax.ppermute(array, 'ctx', swap_z(0))]
    ppermute x8, waiting for transfers between devices: 6.94 us -> 15 us  [swap_odd(): return lax.ppermute(array, 'ctx', swap_z(1))]
    ppermute x3, starting transfers between devices: 4.18 us -> 7.42 us  [on_device(): lax.ppermute(sums[slot].astype(jnp.bfloat16), 'ctx', swap_y(mask))]
    ppermute x8, starting transfers between devices: 19.6 us -> 16.8 us  [swap_odd(): return lax.ppermute(array, 'ctx', swap_z(1))]
  transfers between devices with their start and end apart: 26 -> 26, of which waited for: 15 -> 14; matrix products, arithmetic and copies ran while one was open for 3% -> 3% of each run, Pallas kernels for 29% -> 11%
where the time goes in v3:
time: 98.9 us; the launch traced here: 98.6 us
  waiting for transfers between devices  40.5 us (41%)
  starting transfers between devices  37.2 us (38%)
  Pallas kernels  13.3 us (13%)
  local copies, waits for them, and re-layouts  3.84 us (4%)
  other arithmetic  2.75 us (3%)
  between operations  1 us (1%)
    ppermute x8, waiting for transfers between devices, swap_even(): return lax.ppermute(array, 'ctx', swap_z(0))  19.7 us
    ppermute x8, starting transfers between devices, swap_odd(): return lax.ppermute(array, 'ctx', swap_z(1))  16.8 us
    ppermute x8, waiting for transfers between devices, swap_odd(): return lax.ppermute(array, 'ctx', swap_z(1))  15 us
    pallas_call x9, Pallas kernels, run_stage(): pl.pallas_call(functools.partial(stage_kernel, stage, len(after), len(pas...  13.3 us
    ppermute x3, starting transfers between devices, on_device(): lax.ppermute(sums[slot].astype(jnp.bfloat16), 'ctx', swap_y(mask))  7.42 us
    ppermute x3, starting transfers between devices, on_device(): lax.ppermute(pairs[mask // 2], 'ctx', swap_y(mask))  4.43 us
    unnamed x12, local copies, waits for them, and re-layouts  3.59 us
    ppermute x3, waiting for transfers between devices, on_device(): lax.ppermute(sums[slot].astype(jnp.bfloat16), 'ctx', swap_y(mask))  3.5 us
  transfers between devices with their start and end apart: 26, of which 14 were waited for; matrix products, arithmetic and copies ran while one was open for 3% of the time, Pallas kernels for 11%

profile of v3, /device:TPU:6, one launch (start us, length us, event | category | flops | bytes accessed | tf_op | source)
XLA Modules:
  0.0 98.6 jit_solution(11381785653793257103)
XLA Ops:
  2.5 3.3 %collective-permute-start.3 = (bf16[2,128,128]{2,1,0:T(8,128)(2,1)S(1)}, bf16[2,128,128]{2,1,0:T(8,128)(2,1)S(1)}, u32[]{:S(2)}, u32[]{:S(2)}) collective-permute-start(bf16[2,128,128]{2,1,0:T(8,128)(2,1)S(1)} %pad_maximum_fusion.7), channel_id=1, source_target_pairs={{0,32},{2,34},{4,36},{6,38},{8,40},{10,42},{12,44},{14,46},{16,48}... | collective-permute-start | bytes 196616 | tf_op jit(solution)/shard_map/ppermute | solution.py:327
  7.0 2.3 %collective-permute-start = (bf16[1024,128]{1,0:T(8,128)(2,1)S(1)}, bf16[1024,128]{1,0:T(8,128)(2,1)S(1)}, u32[]{:S(2)}, u32[]{:S(2)}) collective-permute-start(bf16[1024,128]{1,0:T(8,128)(2,1)S(1)} %get-tuple-element.86), channel_id=1, source_target_pairs={{0,48},{2,50},{4,52},{6,54},{8,56},{10,58},{12,60},{14,62},{16,32}... | collective-permute-start | bytes 786440 | tf_op jit(solution)/shard_map/ppermute | solution.py:330
  9.4 1.7 %collective-permute-done.1 = bf16[2,128,128]{2,1,0:T(8,128)(2,1)S(1)} collective-permute-done((bf16[2,128,128]{2,1,0:T(8,128)(2,1)S(1)}, bf16[2,128,128]{2,1,0:T(8,128)(2,1)S(1)}, u32[]{:S(2)}, u32[]{:S(2)}) %collective-permute-start.1) | collective-permute-done | bytes 65568 | tf_op jit(solution)/shard_map/ppermute | solution.py:327
  11.9 2.0 %collective-permute-start.9 = (bf16[4,2,128,128]{3,2,1,0:T(8,128)(2,1)S(1)}, bf16[4,2,128,128]{3,2,1,0:T(8,128)(2,1)S(1)}, u32[]{:S(2)}, u32[]{:S(2)}) collective-permute-start(bf16[4,2,128,128]{3,2,1,0:T(8,128)(2,1)S(1)} %pad_maximum_fusion.2.refs_4_.refs_8_), channel_id=1, source_target_pairs={{0,2},{2,0},{4,6},{6,4},{8,10},{10,8},{12,14},{14,12},{16,18},{18,... | collective-permute-start | bytes 786440 | tf_op jit(solution)/shard_map/ppermute | solution.py:304
  13.9 4.9 %collective-permute-start.5 = (bf16[4,2,128,128]{3,2,1,0:T(8,128)(2,1)S(1)}, bf16[4,2,128,128]{3,2,1,0:T(8,128)(2,1)S(1)}, u32[]{:S(2)}, u32[]{:S(2)}) collective-permute-start(bf16[4,2,128,128]{3,2,1,0:T(8,128)(2,1)S(1)} %pad_maximum_fusion.2.refs_4_.refs_8_), channel_id=1, source_target_pairs={{0,14},{2,4},{4,2},{6,8},{8,6},{10,12},{12,10},{14,0},{16,30},{18,... | collective-permute-start | bytes 786440 | tf_op jit(solution)/shard_map/ppermute | solution.py:308
  19.6 1.8 %fwdown.1 = (f32[2,8,1024]{2,1,0:T(8,128)S(1)}, f32[2,8,1024]{2,1,0:T(8,128)S(1)}, f32[2,128,1024]{2,1,0:T(8,128)S(1)}, bf16[1024,128]{1,0:T(8,128)(2,1)S(1)}) custom-call(s32[16]{0:T(128)S(1)} %copy-done, s32[3]{0:T(128)S(1)} %get-tuple-element.105.refs_1_.refs_3_, ...), custom_call_target="tpu_custom_call", output_to_operand_aliasing={{3}: (5, {})} | custom-call | flops 1610612736 | bytes 4194304 | tf_op jit(solution)/shard_map/fwdown/pallas_call | solution.py:270
  21.4 1.6 %collective-permute-start.4 = (bf16[1024,128]{1,0:T(8,128)(2,1)S(1)}, bf16[1024,128]{1,0:T(8,128)(2,1)S(1)}, u32[]{:S(2)}, u32[]{:S(2)}) collective-permute-start(bf16[1024,128]{1,0:T(8,128)(2,1)S(1)} %get-tuple-element.37), channel_id=1, source_target_pairs={{0,48},{2,50},{4,52},{6,54},{8,56},{10,58},{12,60},{14,62},{16,32}... | collective-permute-start | bytes 786440 | tf_op jit(solution)/shard_map/ppermute | solution.py:349
  23.0 3.4 %collective-permute-start.10 = (bf16[4,2,128,128]{3,2,1,0:T(8,128)(2,1)S(1)}, bf16[4,2,128,128]{3,2,1,0:T(8,128)(2,1)S(1)}, u32[]{:S(2)}, u32[]{:S(2)}) collective-permute-start(bf16[4,2,128,128]{3,2,1,0:T(8,128)(2,1)S(1)} %collective-permute-done.9.refs_4_.refs_8_), channel_id=1, source_target_pairs={{0,14},{2,4},{4,2},{6,8},{8,6},{10,12},{12,10},{14,0},{16,30},{18,... | collective-permute-start | bytes 786440 | tf_op jit(solution)/shard_map/ppermute | solution.py:308
  27.5 3.4 %collective-permute-done.10.refs_5_.refs_9_ = bf16[4,2,128,128]{3,2,1,0:T(8,128)(2,1)S(1)} collective-permute-done((bf16[4,2,128,128]{3,2,1,0:T(8,128)(2,1)S(1)}, bf16[4,2,128,128]{3,2,1,0:T(8,128)(2,1)S(1)}, u32[]{:S(2)}, u32[]{:S(2)}) %collective-permute-start.10) | collective-permute-done | bytes 262176 | tf_op jit(solution)/shard_map/ppermute | solution.py:308
  30.9 3.8 %collective-permute-done.6.refs_4_.refs_8_ = bf16[4,2,128,128]{3,2,1,0:T(8,128)(2,1)S(1)} collective-permute-done((bf16[4,2,128,128]{3,2,1,0:T(8,128)(2,1)S(1)}, bf16[4,2,128,128]{3,2,1,0:T(8,128)(2,1)S(1)}, u32[]{:S(2)}, u32[]{:S(2)}) %collective-permute-start.6) | collective-permute-done | bytes 262176 | tf_op jit(solution)/shard_map/ppermute | solution.py:304
  35.8 2.6 %collective-permute-done.11.refs_4_.refs_6_ = bf16[4,2,128,128]{3,2,1,0:T(8,128)(2,1)S(1)} collective-permute-done((bf16[4,2,128,128]{3,2,1,0:T(8,128)(2,1)S(1)}, bf16[4,2,128,128]{3,2,1,0:T(8,128)(2,1)S(1)}, u32[]{:S(2)}, u32[]{:S(2)}) %collective-permute-start.11) | collective-permute-done | bytes 262176 | tf_op jit(solution)/shard_map/ppermute | solution.py:304
  38.4 2.0 %collective-permute-start.12 = (bf16[2,2,128,128]{3,2,1,0:T(8,128)(2,1)S(1)}, bf16[2,2,128,128]{3,2,1,0:T(8,128)(2,1)S(1)}, u32[]{:S(2)}, u32[]{:S(2)}) collective-permute-start(bf16[2,2,128,128]{3,2,1,0:T(8,128)(2,1)S(1)} %slice.92), channel_id=1, source_target_pairs={{0,14},{2,4},{4,2},{6,8},{8,6},{10,12},{12,10},{14,0},{16,30},{18,... | collective-permute-start | bytes 393224 | tf_op jit(solution)/shard_map/ppermute | solution.py:308
  40.5 3.2 %collective-permute-done.7.refs_5_.refs_7_ = bf16[4,2,128,128]{3,2,1,0:T(8,128)(2,1)S(1)} collective-permute-done((bf16[4,2,128,128]{3,2,1,0:T(8,128)(2,1)S(1)}, bf16[4,2,128,128]{3,2,1,0:T(8,128)(2,1)S(1)}, u32[]{:S(2)}, u32[]{:S(2)}) %collective-permute-start.7) | collective-permute-done | bytes 262176 | tf_op jit(solution)/shard_map/ppermute | solution.py:308
  45.1 3.8 %collective-permute-done.8.refs_6_ = bf16[2,2,128,128]{3,2,1,0:T(8,128)(2,1)S(1)} collective-permute-done((bf16[2,2,128,128]{3,2,1,0:T(8,128)(2,1)S(1)}, bf16[2,2,128,128]{3,2,1,0:T(8,128)(2,1)S(1)}, u32[]{:S(2)}, u32[]{:S(2)}) %collective-permute-start.8) | collective-permute-done | bytes 131104 | tf_op jit(solution)/shard_map/ppermute | solution.py:304
  48.9 2.1 %fwdbwdfar.1 = (bf16[1024,128]{1,0:T(8,128)(2,1)S(1)}, bf16[1024,128]{1,0:T(8,128)(2,1)S(1)}, f32[2,8,1024]{2,1,0:T(8,128)S(1)}, f32[2,8,1024]{2,1,0:T(8,128)S(1...) custom-call(s32[16]{0:T(128)S(1)} %copy-done, ...), custom_call_target="tpu_custom_call" | custom-call | flops 5637144576 | bytes 4194304 | tf_op jit(solution)/shard_map/fwdbwdfar/pallas_call | solution.py:270
  54.3 4.2 %collective-permute-done.14 = bf16[2,2,128,128]{3,2,1,0:T(8,128)(2,1)S(1)} collective-permute-done((bf16[2,2,128,128]{3,2,1,0:T(8,128)(2,1)S(1)}, bf16[2,2,128,128]{3,2,1,0:T(8,128)(2,1)S(1)}, u32[]{:S(2)}, u32[]{:S(2)}) %collective-permute-start.14) | collective-permute-done | bytes 131104 | tf_op jit(solution)/shard_map/ppermute | solution.py:304
  58.5 2.3 %collective-permute-start.15 = (bf16[4,2,128,128]{3,2,1,0:T(8,128)(2,1)S(1)}, bf16[4,2,128,128]{3,2,1,0:T(8,128)(2,1)S(1)}, u32[]{:S(2)}, u32[]{:S(2)}) collective-permute-start(bf16[4,2,128,128]{3,2,1,0:T(8,128)(2,1)S(1)} %pad_maximum_fusion.4.refs_1_), channel_id=1, source_target_pairs={{0,14},{2,4},{4,2},{6,8},{8,6},{10,12},{12,10},{14,0},{16,30},{18,... | collective-permute-start | bytes 786440 | tf_op jit(solution)/shard_map/ppermute | solution.py:308
  62.5 6.4 %collective-permute-done.15 = bf16[4,2,128,128]{3,2,1,0:T(8,128)(2,1)S(1)} collective-permute-done((bf16[4,2,128,128]{3,2,1,0:T(8,128)(2,1)S(1)}, bf16[4,2,128,128]{3,2,1,0:T(8,128)(2,1)S(1)}, u32[]{:S(2)}, u32[]{:S(2)}) %collective-permute-start.15) | collective-permute-done | bytes 262176 | tf_op jit(solution)/shard_map/ppermute | solution.py:308
  69.2 1.8 %collective-permute-start.17 = (bf16[4,2,128,128]{3,2,1,0:T(8,128)(2,1)S(1)}, bf16[4,2,128,128]{3,2,1,0:T(8,128)(2,1)S(1)}, u32[]{:S(2)}, u32[]{:S(2)}) collective-permute-start(bf16[4,2,128,128]{3,2,1,0:T(8,128)(2,1)S(1)} %add_convert_fusion.2.refs_1_), channel_id=1, source_target_pairs={{0,14},{2,4},{4,2},{6,8},{8,6},{10,12},{12,10},{14,0},{16,30},{18,... | collective-permute-start | bytes 786440 | tf_op jit(solution)/shard_map/ppermute | solution.py:308
  72.2 5.2 %collective-permute-done.18 = bf16[4,2,128,128]{3,2,1,0:T(8,128)(2,1)S(1)} collective-permute-done((bf16[4,2,128,128]{3,2,1,0:T(8,128)(2,1)S(1)}, bf16[4,2,128,128]{3,2,1,0:T(8,128)(2,1)S(1)}, u32[]{:S(2)}, u32[]{:S(2)}) %collective-permute-start.18) | collective-permute-done | bytes 262176 | tf_op jit(solution)/shard_map/ppermute | solution.py:304
  78.9 2.4 %bwdown.1 = (bf16[1024,128]{1,0:T(8,128)(2,1)S(1)}, bf16[1024,128]{1,0:T(8,128)(2,1)S(1)}, bf16[4,2,128,128]{3,2,1,0:T(8,128)(2,1)S(1)}, bf16[1024,128]{1,0:T(8,128)(2,1)S(1)}) custom-call(bf16[4,2,128,128]{3,2,1,0:T(8,128)(2,1)S(1)} %add_convert_fusion.1.refs_0_, ...), custom_call_target="tpu_custom_call", output_to_operand_aliasing={{3}: (12, {})} | custom-call | flops 4026531840 | bytes 4194304 | tf_op jit(solution)/shard_map/bwdown/pallas_call | solution.py:270
  83.2 2.0 %collective-permute-done.22 = bf16[4,2,128,128]{3,2,1,0:T(8,128)(2,1)S(1)} collective-permute-done((bf16[4,2,128,128]{3,2,1,0:T(8,128)(2,1)S(1)}, bf16[4,2,128,128]{3,2,1,0:T(8,128)(2,1)S(1)}, u32[]{:S(2)}, u32[]{:S(2)}) %collective-permute-start.22) | collective-permute-done | bytes 262176 | tf_op jit(solution)/shard_map/ppermute | solution.py:308
  85.3 6.4 %collective-permute-start.23 = (bf16[2,128,128]{2,1,0:T(8,128)(2,1)S(1)}, bf16[2,128,128]{2,1,0:T(8,128)(2,1)S(1)}, u32[]{:S(2)}, u32[]{:S(2)}) collective-permute-start(bf16[2,128,128]{2,1,0:T(8,128)(2,1)S(1)} %get-tuple-element.88), channel_id=1, source_target_pairs={{0,32},{2,34},{4,36},{6,38},{8,40},{10,42},{12,44},{14,46},{16,48}... | collective-permute-start | bytes 196616 | tf_op jit(solution)/shard_map/ppermute | solution.py:382
  93.9 2.0 %collective-permute-done.25 = bf16[2,128,128]{2,1,0:T(8,128)(2,1)S(1)} collective-permute-done((bf16[2,128,128]{2,1,0:T(8,128)(2,1)S(1)}, bf16[2,128,128]{2,1,0:T(8,128)(2,1)S(1)}, u32[]{:S(2)}, u32[]{:S(2)}) %collective-permute-start.25) | collective-permute-done | bytes 65568 | tf_op jit(solution)/shard_map/ppermute | solution.py:382
  (79 shorter events, 22.9 us)
Async XLA Ops:
  2.5 8.7 %collective-permute-start.3 = (bf16[2,128,128]{2,1,0:T(8,128)(2,1)S(1)}, bf16[2,128,128]{2,1,0:T(8,128)(2,1)S(1)}, u32[]{:S(2)}, u32[]{:S(2)}) collective-permute-start(bf16[2,128,128]{2,1,0:T(8,128)(2,1)S(1)} %pad_maximum_fusion.7), channel_id=1, source_target_pairs={{0,32},{2,34},{4,36},{6,38},{8,40},{10,42},{12,44},{14,46},{16,48}... | collective-permute-start | bytes 196616 | tf_op jit(solution)/shard_map/ppermute | solution.py:327
  5.7 6.1 %collective-permute-start.2 = (bf16[2,128,128]{2,1,0:T(8,128)(2,1)S(1)}, bf16[2,128,128]{2,1,0:T(8,128)(2,1)S(1)}, u32[]{:S(2)}, u32[]{:S(2)}) collective-permute-start(bf16[2,128,128]{2,1,0:T(8,128)(2,1)S(1)} %pad_maximum_fusion.7), channel_id=1, source_target_pairs={{0,48},{2,50},{4,52},{6,54},{8,56},{10,58},{12,60},{14,62},{16,32}... | collective-permute-start | bytes 196616 | tf_op jit(solution)/shard_map/ppermute | solution.py:327
  7.0 11.9 %collective-permute-start = (bf16[1024,128]{1,0:T(8,128)(2,1)S(1)}, bf16[1024,128]{1,0:T(8,128)(2,1)S(1)}, u32[]{:S(2)}, u32[]{:S(2)}) collective-permute-start(bf16[1024,128]{1,0:T(8,128)(2,1)S(1)} %get-tuple-element.86), channel_id=1, source_target_pairs={{0,48},{2,50},{4,52},{6,54},{8,56},{10,58},{12,60},{14,62},{16,32}... | collective-permute-start | bytes 786440 | tf_op jit(solution)/shard_map/ppermute | solution.py:330
  11.9 11.2 %collective-permute-start.9 = (bf16[4,2,128,128]{3,2,1,0:T(8,128)(2,1)S(1)}, bf16[4,2,128,128]{3,2,1,0:T(8,128)(2,1)S(1)}, u32[]{:S(2)}, u32[]{:S(2)}) collective-permute-start(bf16[4,2,128,128]{3,2,1,0:T(8,128)(2,1)S(1)} %pad_maximum_fusion.2.refs_4_.refs_8_), channel_id=1, source_target_pairs={{0,2},{2,0},{4,6},{6,4},{8,10},{10,8},{12,14},{14,12},{16,18},{18,... | collective-permute-start | bytes 786440 | tf_op jit(solution)/shard_map/ppermute | solution.py:304
  13.9 12.5 %collective-permute-start.5 = (bf16[4,2,128,128]{3,2,1,0:T(8,128)(2,1)S(1)}, bf16[4,2,128,128]{3,2,1,0:T(8,128)(2,1)S(1)}, u32[]{:S(2)}, u32[]{:S(2)}) collective-permute-start(bf16[4,2,128,128]{3,2,1,0:T(8,128)(2,1)S(1)} %pad_maximum_fusion.2.refs_4_.refs_8_), channel_id=1, source_target_pairs={{0,14},{2,4},{4,2},{6,8},{8,6},{10,12},{12,10},{14,0},{16,30},{18,... | collective-permute-start | bytes 786440 | tf_op jit(solution)/shard_map/ppermute | solution.py:308
  21.4 23.7 %collective-permute-start.4 = (bf16[1024,128]{1,0:T(8,128)(2,1)S(1)}, bf16[1024,128]{1,0:T(8,128)(2,1)S(1)}, u32[]{:S(2)}, u32[]{:S(2)}) collective-permute-start(bf16[1024,128]{1,0:T(8,128)(2,1)S(1)} %get-tuple-element.37), channel_id=1, source_target_pairs={{0,48},{2,50},{4,52},{6,54},{8,56},{10,58},{12,60},{14,62},{16,32}... | collective-permute-start | bytes 786440 | tf_op jit(solution)/shard_map/ppermute | solution.py:349
  23.0 7.9 %collective-permute-start.10 = (bf16[4,2,128,128]{3,2,1,0:T(8,128)(2,1)S(1)}, bf16[4,2,128,128]{3,2,1,0:T(8,128)(2,1)S(1)}, u32[]{:S(2)}, u32[]{:S(2)}) collective-permute-start(bf16[4,2,128,128]{3,2,1,0:T(8,128)(2,1)S(1)} %collective-permute-done.9.refs_4_.refs_8_), channel_id=1, source_target_pairs={{0,14},{2,4},{4,2},{6,8},{8,6},{10,12},{12,10},{14,0},{16,30},{18,... | collective-permute-start | bytes 786440 | tf_op jit(solution)/shard_map/ppermute | solution.py:308
  26.4 8.3 %collective-permute-start.6 = (bf16[4,2,128,128]{3,2,1,0:T(8,128)(2,1)S(1)}, bf16[4,2,128,128]{3,2,1,0:T(8,128)(2,1)S(1)}, u32[]{:S(2)}, u32[]{:S(2)}) collective-permute-start(bf16[4,2,128,128]{3,2,1,0:T(8,128)(2,1)S(1)} %collective-permute-done.5.refs_5_.refs_9_), channel_id=1, source_target_pairs={{0,2},{2,0},{4,6},{6,4},{8,10},{10,8},{12,14},{14,12},{16,18},{18,... | collective-permute-start | bytes 786440 | tf_op jit(solution)/shard_map/ppermute | solution.py:304
  30.9 7.5 %collective-permute-start.11 = (bf16[4,2,128,128]{3,2,1,0:T(8,128)(2,1)S(1)}, bf16[4,2,128,128]{3,2,1,0:T(8,128)(2,1)S(1)}, u32[]{:S(2)}, u32[]{:S(2)}) collective-permute-start(bf16[4,2,128,128]{3,2,1,0:T(8,128)(2,1)S(1)} %collective-permute-done.10.refs_5_.refs_9_), channel_id=1, source_target_pairs={{0,2},{2,0},{4,6},{6,4},{8,10},{10,8},{12,14},{14,12},{16,18},{18,... | collective-permute-start | bytes 786440 | tf_op jit(solution)/shard_map/ppermute | solution.py:304
  34.7 9.0 %collective-permute-start.7 = (bf16[4,2,128,128]{3,2,1,0:T(8,128)(2,1)S(1)}, bf16[4,2,128,128]{3,2,1,0:T(8,128)(2,1)S(1)}, u32[]{:S(2)}, u32[]{:S(2)}) collective-permute-start(bf16[4,2,128,128]{3,2,1,0:T(8,128)(2,1)S(1)} %collective-permute-done.6.refs_4_.refs_8_), channel_id=1, source_target_pairs={{0,14},{2,4},{4,2},{6,8},{8,6},{10,12},{12,10},{14,0},{16,30},{18,... | collective-permute-start | bytes 786440 | tf_op jit(solution)/shard_map/ppermute | solution.py:308
  38.4 6.7 %collective-permute-start.12 = (bf16[2,2,128,128]{3,2,1,0:T(8,128)(2,1)S(1)}, bf16[2,2,128,128]{3,2,1,0:T(8,128)(2,1)S(1)}, u32[]{:S(2)}, u32[]{:S(2)}) collective-permute-start(bf16[2,2,128,128]{3,2,1,0:T(8,128)(2,1)S(1)} %slice.92), channel_id=1, source_target_pairs={{0,14},{2,4},{4,2},{6,8},{8,6},{10,12},{12,10},{14,0},{16,30},{18,... | collective-permute-start | bytes 393224 | tf_op jit(solution)/shard_map/ppermute | solution.py:308
  43.7 5.2 %collective-permute-start.8 = (bf16[2,2,128,128]{3,2,1,0:T(8,128)(2,1)S(1)}, bf16[2,2,128,128]{3,2,1,0:T(8,128)(2,1)S(1)}, u32[]{:S(2)}, u32[]{:S(2)}) collective-permute-start(bf16[2,2,128,128]{3,2,1,0:T(8,128)(2,1)S(1)} %slice.91), channel_id=1, source_target_pairs={{0,2},{2,0},{4,6},{6,4},{8,10},{10,8},{12,14},{14,12},{16,18},{18,... | collective-permute-start | bytes 393224 | tf_op jit(solution)/shard_map/ppermute | solution.py:304
  51.0 9.9 %collective-permute-start.13 = (bf16[2,2,128,128]{3,2,1,0:T(8,128)(2,1)S(1)}, bf16[2,2,128,128]{3,2,1,0:T(8,128)(2,1)S(1)}, u32[]{:S(2)}, u32[]{:S(2)}) collective-permute-start(bf16[2,2,128,128]{3,2,1,0:T(8,128)(2,1)S(1)} %get-tuple-element.55), channel_id=1, source_target_pairs={{0,14},{2,4},{4,2},{6,8},{8,6},{10,12},{12,10},{14,0},{16,30},{18,... | collective-permute-start | bytes 393224 | tf_op jit(solution)/shard_map/ppermute | solution.py:308
  52.2 6.3 %collective-permute-start.14 = (bf16[2,2,128,128]{3,2,1,0:T(8,128)(2,1)S(1)}, bf16[2,2,128,128]{3,2,1,0:T(8,128)(2,1)S(1)}, u32[]{:S(2)}, u32[]{:S(2)}) collective-permute-start(bf16[2,2,128,128]{3,2,1,0:T(8,128)(2,1)S(1)} %get-tuple-element.57), channel_id=1, source_target_pairs={{0,2},{2,0},{4,6},{6,4},{8,10},{10,8},{12,14},{14,12},{16,18},{18,... | collective-permute-start | bytes 393224 | tf_op jit(solution)/shard_map/ppermute | solution.py:304
  52.2 26.7 %collective-permute-start.19 = (bf16[1024,128]{1,0:T(8,128)(2,1)S(1)}, bf16[1024,128]{1,0:T(8,128)(2,1)S(1)}, u32[]{:S(2)}, u32[]{:S(2)}) collective-permute-start(bf16[1024,128]{1,0:T(8,128)(2,1)S(1)} %get-tuple-element.65), channel_id=1, source_target_pairs={{0,48},{2,50},{4,52},{6,54},{8,56},{10,58},{12,60},{14,62},{16,32}... | collective-permute-start | bytes 786440 | tf_op jit(solution)/shard_map/ppermute | solution.py:356
  58.5 10.4 %collective-permute-start.15 = (bf16[4,2,128,128]{3,2,1,0:T(8,128)(2,1)S(1)}, bf16[4,2,128,128]{3,2,1,0:T(8,128)(2,1)S(1)}, u32[]{:S(2)}, u32[]{:S(2)}) collective-permute-start(bf16[4,2,128,128]{3,2,1,0:T(8,128)(2,1)S(1)} %pad_maximum_fusion.4.refs_1_), channel_id=1, source_target_pairs={{0,14},{2,4},{4,2},{6,8},{8,6},{10,12},{12,10},{14,0},{16,30},{18,... | collective-permute-start | bytes 786440 | tf_op jit(solution)/shard_map/ppermute | solution.py:308
  60.9 8.1 %collective-permute-start.16 = (bf16[4,2,128,128]{3,2,1,0:T(8,128)(2,1)S(1)}, bf16[4,2,128,128]{3,2,1,0:T(8,128)(2,1)S(1)}, u32[]{:S(2)}, u32[]{:S(2)}) collective-permute-start(bf16[4,2,128,128]{3,2,1,0:T(8,128)(2,1)S(1)} %pad_maximum_fusion.3.refs_0_), channel_id=1, source_target_pairs={{0,2},{2,0},{4,6},{6,4},{8,10},{10,8},{12,14},{14,12},{16,18},{18,... | collective-permute-start | bytes 786440 | tf_op jit(solution)/shard_map/ppermute | solution.py:304
  69.0 8.4 %collective-permute-start.18 = (bf16[4,2,128,128]{3,2,1,0:T(8,128)(2,1)S(1)}, bf16[4,2,128,128]{3,2,1,0:T(8,128)(2,1)S(1)}, u32[]{:S(2)}, u32[]{:S(2)}) collective-permute-start(bf16[4,2,128,128]{3,2,1,0:T(8,128)(2,1)S(1)} %add_convert_fusion.3.refs_0_), channel_id=1, source_target_pairs={{0,2},{2,0},{4,6},{6,4},{8,10},{10,8},{12,14},{14,12},{16,18},{18,... | collective-permute-start | bytes 786440 | tf_op jit(solution)/shard_map/ppermute | solution.py:304
  69.2 9.5 %collective-permute-start.17 = (bf16[4,2,128,128]{3,2,1,0:T(8,128)(2,1)S(1)}, bf16[4,2,128,128]{3,2,1,0:T(8,128)(2,1)S(1)}, u32[]{:S(2)}, u32[]{:S(2)}) collective-permute-start(bf16[4,2,128,128]{3,2,1,0:T(8,128)(2,1)S(1)} %add_convert_fusion.2.refs_1_), channel_id=1, source_target_pairs={{0,14},{2,4},{4,2},{6,8},{8,6},{10,12},{12,10},{14,0},{16,30},{18,... | collective-permute-start | bytes 786440 | tf_op jit(solution)/shard_map/ppermute | solution.py:308
  77.5 7.7 %collective-permute-start.22 = (bf16[4,2,128,128]{3,2,1,0:T(8,128)(2,1)S(1)}, bf16[4,2,128,128]{3,2,1,0:T(8,128)(2,1)S(1)}, u32[]{:S(2)}, u32[]{:S(2)}) collective-permute-start(bf16[4,2,128,128]{3,2,1,0:T(8,128)(2,1)S(1)} %add_convert_fusion.refs_1_), channel_id=1, source_target_pairs={{0,14},{2,4},{4,2},{6,8},{8,6},{10,12},{12,10},{14,0},{16,30},{18,... | collective-permute-start | bytes 786440 | tf_op jit(solution)/shard_map/ppermute | solution.py:308
  78.7 6.5 %collective-permute-start.21 = (bf16[4,2,128,128]{3,2,1,0:T(8,128)(2,1)S(1)}, bf16[4,2,128,128]{3,2,1,0:T(8,128)(2,1)S(1)}, u32[]{:S(2)}, u32[]{:S(2)}) collective-permute-start(bf16[4,2,128,128]{3,2,1,0:T(8,128)(2,1)S(1)} %add_convert_fusion.1.refs_0_), channel_id=1, source_target_pairs={{0,2},{2,0},{4,6},{6,4},{8,10},{10,8},{12,14},{14,12},{16,18},{18,... | collective-permute-start | bytes 786440 | tf_op jit(solution)/shard_map/ppermute | solution.py:304
  81.4 11.4 %collective-permute-start.20 = (bf16[1024,128]{1,0:T(8,128)(2,1)S(1)}, bf16[1024,128]{1,0:T(8,128)(2,1)S(1)}, u32[]{:S(2)}, u32[]{:S(2)}) collective-permute-start(bf16[1024,128]{1,0:T(8,128)(2,1)S(1)} %get-tuple-element.68), channel_id=1, source_target_pairs={{0,48},{2,50},{4,52},{6,54},{8,56},{10,58},{12,60},{14,62},{16,32}... | collective-permute-start | bytes 786440 | tf_op jit(solution)/shard_map/ppermute | solution.py:373
  85.3 8.6 %collective-permute-start.23 = (bf16[2,128,128]{2,1,0:T(8,128)(2,1)S(1)}, bf16[2,128,128]{2,1,0:T(8,128)(2,1)S(1)}, u32[]{:S(2)}, u32[]{:S(2)}) collective-permute-start(bf16[2,128,128]{2,1,0:T(8,128)(2,1)S(1)} %get-tuple-element.88), channel_id=1, source_target_pairs={{0,32},{2,34},{4,36},{6,38},{8,40},{10,42},{12,44},{14,46},{16,48}... | collective-permute-start | bytes 196616 | tf_op jit(solution)/shard_map/ppermute | solution.py:382
  91.7 5.5 %collective-permute-start.24 = (bf16[2,128,128]{2,1,0:T(8,128)(2,1)S(1)}, bf16[2,128,128]{2,1,0:T(8,128)(2,1)S(1)}, u32[]{:S(2)}, u32[]{:S(2)}) collective-permute-start(bf16[2,128,128]{2,1,0:T(8,128)(2,1)S(1)} %get-tuple-element.90), channel_id=1, source_target_pairs={{0,48},{2,50},{4,52},{6,54},{8,56},{10,58},{12,60},{14,62},{16,32}... | collective-permute-start | bytes 196616 | tf_op jit(solution)/shard_map/ppermute | solution.py:382
  (7 other events, 18.1 us)
